TPU v7x, 256 devices: a whole 4x4x8 slice. The times are simulated.
256 devices in a mesh: tm: 8 (over z), chan: 32 (over y, x, core).
Axes of the slice: x: 4, y: 4, z: 8, core: 2. Of those that a mesh axis runs over, the one named last changes fastest.
Arguments:
- raw_traces: bfloat16 [49152, 4096], P('tm', 'chan'), may hold values from -18 to 18
Outputs:
- cross_spectra: bfloat16 [32, 2, 4096, 4096], P('tm', None, 'chan')
All inputs are finite; a program needn't handle non-finite values.
Results may differ from a plain program's by a relative error of at most 0.0077.
Values may be sent and summed in bfloat16 or wider, within the bound.
A program may use at most 64 MiB of HBM per device.

v0:
```python
import math

import jax
import jax.numpy as jnp
from jax import lax
from jax.sharding import PartitionSpec as P

NFFT = 1024
NBINS = 32
SMOOTH = 4
BAND_START = 64


FLOOR_FRACTION = 0.125


def passed_along(x, axis, by):
    count = lax.axis_size(axis)
    pairs = [(i, i + by) for i in range(count) if 0 <= i + by < count]
    return lax.ppermute(x, axis, pairs)


def spectral_table():
    span_bins = NBINS + 2 * SMOOTH
    sample = jnp.arange(NFFT, dtype=jnp.int32)
    band_bins = BAND_START - SMOOTH + jnp.arange(span_bins, dtype=jnp.int32)
    phase_turns = sample[:, None] * band_bins[None, :] % NFFT
    angles = phase_turns.astype(jnp.float32) * (2.0 * math.pi / NFFT)
    return jnp.concatenate([jnp.cos(angles), -jnp.sin(angles)], axis=1).astype(jnp.bfloat16)


def taper():
    sample = jnp.arange(NFFT, dtype=jnp.float32)
    return 0.5 - 0.5 * jnp.cos(sample * (2.0 * math.pi / NFFT))


def whiten(spectra):
    span_bins = NBINS + 2 * SMOOTH
    real_part = spectra[:, :span_bins]
    imag_part = spectra[:, span_bins:]
    magnitude = jnp.sqrt(real_part * real_part + imag_part * imag_part)
    smoothed = magnitude[:, 0:NBINS]
    for offset in range(1, 2 * SMOOTH + 1):
        smoothed = smoothed + magnitude[:, offset : offset + NBINS]
    smoothed = smoothed / (2 * SMOOTH + 1)
    factor = 1.0 / jnp.maximum(smoothed, FLOOR_FRACTION * math.sqrt(NFFT))
    band_real = real_part[:, SMOOTH : SMOOTH + NBINS] * factor
    band_imag = imag_part[:, SMOOTH : SMOOTH + NBINS] * factor
    return jnp.stack([band_real, band_imag], axis=1).astype(jnp.bfloat16)


def cross_block(own_rows, piece, frames_all):
    rotated = jnp.stack([-piece[:, 1], piece[:, 0]], axis=1)
    partner = jnp.stack([piece, rotated], axis=3)
    products = jnp.einsum("kpgr,kpgoc->gorc", own_rows, partner, preferred_element_type=jnp.float32)
    return (products / frames_all).astype(jnp.bfloat16)


def local(raw_traces):
    hop_len = NFFT // 2
    width_ch = raw_traces.shape[1]
    frames_dev = raw_traces.shape[0] // hop_len
    table = spectral_table()
    window_taper = taper()
    pieces = raw_traces.reshape(frames_dev, hop_len, width_ch)
    following = passed_along(pieces[0], "tm", -1)
    extended = jnp.concatenate([pieces, following[None]], axis=0)
    frames = jnp.concatenate([extended[:-1], extended[1:]], axis=1)
    windowed = (frames.astype(jnp.float32) * window_taper[None, :, None]).astype(jnp.bfloat16)
    spectra = jnp.einsum("nf,knc->kfc", table, windowed, preferred_element_type=jnp.float32)
    whitened = whiten(spectra)
    everyone = lax.all_gather(whitened, "chan", axis=3, tiled=True)
    grouped_all = lax.all_to_all(everyone, "tm", split_axis=2, concat_axis=0, tiled=True)
    frames_all = float(grouped_all.shape[0])
    own_rows = lax.dynamic_slice_in_dim(grouped_all, lax.axis_index("chan") * width_ch, width_ch, 3)
    return cross_block(own_rows, grouped_all, frames_all)


def solution(mesh):
    placed = (P("tm", "chan"),)
    return jax.shard_map(
        local, mesh=mesh, in_specs=placed, out_specs=P("tm", None, "chan", None), check_vma=False
    )
```

profile of v0, /device:TPU:1, one launch (start us, length us, event | category | flops | bytes accessed | tf_op | source)
XLA Modules:
  0.0 306.7 jit_solution(12502554316319397357)
XLA Ops:
  6.5 0.0 all-gather.2.cloned.1.call-start
  6.5 0.9 slice.54
  7.5 1.3 collective-permute-start
  8.8 0.7 cosine_convert_fusion
  9.5 4.6 %collective-permute-done = bf16[512,128]{1,0:T(8,128)(2,1)S(1)} collective-permute-done((bf16[512,128]{1,0:T(8,128)(2,1)S(1)}, bf16[512,128]{1,0:T(8,128)(2,1)S(1)}, u32[]{:S(2)}, u32[]{:S(2)}) %collective-permute-start) | collective-permute-done | bytes 131104 | tf_op jit(solution)/shard_map/ppermute | solution.py:20
  14.2 2.7 fusion.14
  16.9 0.1 fusion.16
  16.9 0.2 fusion.30
  17.2 0.7 pad_maximum_fusion.1
  17.9 0.0 all-gather.2.cloned.1.call-update
  17.9 64.1 %all-gather.2.cloned.1.call-done = bf16[12,2,32,4096]{3,2,0,1:T(8,128)(2,1)} async-done(((bf16[12,2,32,128]{3,2,0,1:T(8,128)(2,1)}), bf16[12,2,32,4096]{3,2,0,1:T(8,128)(2,1)}) %all-gather.2.cloned.1.call-update) | async-done | bytes 6291472 | tf_op jit(solution)/shard_map/all_gather | solution.py:72
  82.1 12.7 %copy.19 = bf16[12,2,32,4096]{3,1,0,2:T(2,128)(2,1)} copy(bf16[12,2,32,4096]{3,2,0,1:T(8,128)(2,1)} %all-gather.2.cloned.1.call-done) | data formatting | bytes 12582912 | tf_op jit(solution)/shard_map/all_gather | solution.py:72
  94.7 6.7 %all-to-all-start = ((bf16[12,2,32,4096]{3,1,0,2:T(2,128)(2,1)}), bf16[12,2,32,4096]{3,1,0,2:T(2,128)(2,1)}, u32[]{:S(2)}, u32[]{:S(2)}) async-start(bf16[12,2,32,4096]{3,1,0,2:T(2,128)(2,1)} %copy.19), calls=%async_computation | async-start | bytes 12582912 | tf_op jit(solution)/shard_map/all_to_all | solution.py:73
  101.5 142.0 %all-to-all-done = bf16[12,2,32,4096]{3,1,0,2:T(2,128)(2,1)} async-done(((bf16[12,2,32,4096]{3,1,0,2:T(2,128)(2,1)}), bf16[12,2,32,4096]{3,1,0,2:T(2,128)(2,1)}, u32[]{:S(2)}, u32[]{:S(2)}) %all-to-all-start) | async-done | bytes 6291488 | tf_op jit(solution)/shard_map/all_to_all | solution.py:73
  243.4 15.6 %copy.20 = bf16[12,2,8,4,4096]{4,3,1,0,2:T(4,128)(2,1)S(1)} copy(bf16[12,2,8,4,4096]{4,1,0,3,2:T(2,128)(2,1)} %bitcast.6) | data formatting | bytes 12582912 | tf_op jit(solution)/shard_map/all_to_all | solution.py:73
  259.1 2.8 fusion.35
  261.9 0.1 constant_dynamic-slice_fusion
  262.0 6.1 %copy.23 = bf16[96,2,4,1,4096]{4,0,1,3,2:T(8,128)(2,1)} copy(bf16[96,2,4,1,4096]{4,2,1,0,3:T(4,128)(2,1)S(1)} %bitcast.35) | data formatting | bytes 12582912 | tf_op jit(solution)/shard_map/stack | solution.py:54
  268.1 3.6 %copy_negate_fusion = bf16[96,1,4,4096]{3,0,1,2:T(8,128)(2,1)S(1)} fusion(bf16[96,1,4,4096]{3,2,1,0:T(4,128)(2,1)S(1)} %get-tuple-element.7), kind=kLoop, calls=%fused_computation.14 | loop fusion | flops 1572864 | bytes 6291456 | tf_op jit(solution)/shard_map/neg | solution.py:53
  271.7 0.0 slice-start
  271.7 1.7 copy.29
  273.5 0.0 slice-start.1
  273.5 3.3 %maximum_bitcast_fusion = bf16[96,2,4,1,4096]{4,0,1,3,2:T(8,128)(2,1)} fusion(bf16[96,1,4,4096]{3,0,1,2:T(8,128)(2,1)S(1)} %copy.29, bf16[96,1,4,4096]{3,0,1,2:T(8,128)(2,1)S(1)} %copy_negate_fusion), kind=kLoop, calls=%fused_computation.7 | loop fusion | flops 3145728 | bytes 12582912 | tf_op jit(solution)/shard_map/stack | solution.py:54
  276.7 0.0 slice-done
  276.7 0.0 slice-done.1
  276.7 11.1 %fusion.5 = bf16[4,2,128,4096]{2,3,1,0:T(8,128)(2,1)} fusion(bf16[96,2,4,1,4096]{4,0,1,3,2:T(8,128)(2,1)} %maximum_bitcast_fusion, bf16[96,2,4,1,4096]{4,0,1,3,2:T(8,128)(2,1)S(1)} %bitcast.37, bf16[96,2,4,128]{3,2,1,0:T(4,128)(2,1)S(1)} %constant_dynamic-slice_fusion), kind=kOutput, calls=%fused_computation.6 | convolution fusion | flops 1625292800 | bytes 21168128 | tf_op jit(solution)/shard_map/kpgr,kpgoc->gorc/dot_general | solution.py:55
  287.9 12.0 %copy.25 = bf16[4,2,128,4096]{3,2,1,0:T(8,128)(2,1)} copy(bf16[4,2,128,4096]{2,3,1,0:T(8,128)(2,1)} %fusion.5) | data formatting | bytes 16777216 | tf_op jit(solution)/shard_map/convert_element_type | solution.py:56
  (4 shorter events, 0.1 us)
Async XLA Ops:
  6.5 75.5 %all-gather.2.cloned.1.call-start = ((), (), s32[]{:S(2)}) async-start(), calls=%async_computation.1 | async-start | bytes 6488064 | tf_op jit(solution)/shard_map/all_gather | solution.py:72
  7.5 6.7 %collective-permute-start = (bf16[512,128]{1,0:T(8,128)(2,1)S(1)}, bf16[512,128]{1,0:T(8,128)(2,1)S(1)}, u32[]{:S(2)}, u32[]{:S(2)}) collective-permute-start(bf16[512,128]{1,0:T(8,128)(2,1)S(1)} %slice.54), channel_id=1, source_target_pairs={{32,0},{64,32},{96,64},{128,96},{160,128},{192,160},{224,192},{33,... | collective-permute-start | bytes 393224 | tf_op jit(solution)/shard_map/ppermute | solution.py:20
  94.7 148.7 %all-to-all-start = ((bf16[12,2,32,4096]{3,1,0,2:T(2,128)(2,1)}), bf16[12,2,32,4096]{3,1,0,2:T(2,128)(2,1)}, u32[]{:S(2)}, u32[]{:S(2)}) async-start(bf16[12,2,32,4096]{3,1,0,2:T(2,128)(2,1)} %copy.19), calls=%async_computation | async-start | bytes 12582912 | tf_op jit(solution)/shard_map/all_to_all | solution.py:73
  271.7 5.0 %slice-start = ((s8[6291456]{0:T(1024)(128)(4,1)}), s8[4194304]{0:T(1024)(128)(4,1)S(1)}, s32[]{:S(2)}) async-start(s8[6291456]{0:T(1024)(128)(4,1)} %bitcast.36), calls=%async_computation.2 | async-start | bytes 8388608
  273.5 3.3 %slice-start.1 = ((s8[6291456]{0:T(1024)(128)(4,1)}), s8[2097152]{0:T(1024)(128)(4,1)S(1)}, s32[]{:S(2)}) async-start(s8[6291456]{0:T(1024)(128)(4,1)} %bitcast.36), calls=%async_computation.3 | async-start | bytes 4194304
Sparse Core Ops, SparseCore 0:
  18.0 63.9 all-gather.1
where the time goes:
time: 307 us
  waiting for transfers between devices  211 us (69%)
  local copies, waits for them, and re-layouts  51.9 us (17%)
  matrix products  13.8 us (4%)
  between operations  13.5 us (4%)
  other arithmetic  8.71 us (3%)
  starting transfers between devices  8.03 us (3%)
    all_to_all x1, waiting for transfers between devices, local(): lax.all_to_all(everyone, 'tm', split_axis=2, concat_axis=0, tiled=True)  142 us
    all_gather x1, waiting for transfers between devices, local(): everyone = lax.all_gather(whitened, 'chan', axis=3, tiled=True)  64.1 us
    all_to_all x1, local copies, waits for them, and re-layouts, local(): lax.all_to_all(everyone, 'tm', split_axis=2, concat_axis=0, tiled=True)  15.6 us
    all_gather x1, local copies, waits for them, and re-layouts, local(): everyone = lax.all_gather(whitened, 'chan', axis=3, tiled=True)  12.7 us
    convert_element_type x1, local copies, waits for them, and re-layouts, cross_block(): return (products / frames_all).astype(jnp.bfloat16)  12 us
    dot_general x1, matrix products, cross_block(): jnp.einsum('kpgr,kpgoc->gorc', own_rows, partner, preferred_element_type=...  11.1 us
    all_to_all x1, starting transfers between devices, local(): lax.all_to_all(everyone, 'tm', split_axis=2, concat_axis=0, tiled=True)  6.73 us
  transfers between devices with their start and end apart: 3, of which 3 were waited for; matrix products, arithmetic and copies ran while one was open for 0% of the time, Pallas kernels for 0%

commit v1 on v0

v1 whole, which is shorter than its diff:
```python
import functools
import math

import jax
import jax.numpy as jnp
import numpy as np
from jax import lax
from jax.experimental import pallas as pl
from jax.experimental.pallas import tpu as pltpu
from jax.sharding import PartitionSpec as P

NFFT = 1024
HOP = NFFT // 2
NBINS = 32
SMOOTH = 4
BAND_START = 64
SPAN = NBINS + 2 * SMOOTH
FLOOR = 0.125 * math.sqrt(NFFT)
TM = 8
SIDE = 4
CORES = 2
CH = 128
PIECES = 12
FRAMES = TM * PIECES
GROUP = NBINS // TM
ROWS = 2 * PIECES
DEPTH = ROWS * TM
BATCH = GROUP // 2
MESH = pl.DeviceIdType.MESH
F32 = jnp.float32
BF16 = jnp.bfloat16


def spectral_table():
    sample = np.arange(NFFT)
    bins = BAND_START - SMOOTH + np.arange(SPAN)
    angles = (sample[:, None] * bins[None, :] % NFFT).astype(np.float64) * (2.0 * math.pi / NFFT)
    table = np.concatenate([np.cos(angles), -np.sin(angles)], axis=1).astype(np.float32)
    halves = np.concatenate([table[:HOP].T, table[HOP:].T], axis=0)
    return halves.astype(jnp.bfloat16)


def taper_half():
    sample = np.arange(HOP, dtype=np.float64)
    half = 0.5 - 0.5 * np.cos(sample * (2.0 * math.pi / NFFT))
    return np.broadcast_to(half.astype(np.float32)[:, None], (HOP, CH)).copy()


def whiten(spectra):
    real, imag = spectra[:SPAN], spectra[SPAN:]
    magnitude = jnp.sqrt(real * real + imag * imag)
    two = magnitude + pltpu.roll(magnitude, SPAN - 1, 0)
    four = two + pltpu.roll(two, SPAN - 2, 0)
    eight = four + pltpu.roll(four, SPAN - 4, 0)
    nine = eight + pltpu.roll(magnitude, SPAN - 8, 0)
    factor = 1.0 / jnp.maximum(nine * (1.0 / (2 * SMOOTH + 1)), FLOOR)
    factor = pltpu.roll(factor, SMOOTH, 0)
    return real * factor, imag * factor


def gather_kernel(
    raw_hbm, table_hbm, taper_hbm, gathered, own_t,
    raw, table, taper, spec, halo_out, halo_in, white, to_tm, from_tm,
    load_sem, halo_sem, tm_send, tm_recv, ici_send, ici_recv, sib_send, sib_recv,
):
    z = lax.axis_index("tm")
    chan = lax.axis_index("chan")
    core = lax.rem(chan, CORES)
    place = chan // CORES
    y, x = place // SIDE, lax.rem(place, SIDE)

    def chan_of(yy, xx, cc):
        return (lax.rem(yy + SIDE, SIDE) * SIDE + lax.rem(xx + SIDE, SIDE)) * CORES + cc

    def place_of(dy, dx):
        return lax.rem(y + dy + SIDE, SIDE) * SIDE + lax.rem(x + dx + SIDE, SIDE)

    sibling = chan_of(y, x, 1 - core)

    chunks = [(0, 1), (1, 3), (4, 4), (8, 4)]
    loads = [
        pltpu.make_async_copy(table_hbm, table, load_sem.at[0]),
        pltpu.make_async_copy(taper_hbm, taper, load_sem.at[1]),
    ]
    for i, (first, count) in enumerate(chunks):
        part = pl.ds(first * HOP, count * HOP)
        loads.append(pltpu.make_async_copy(raw_hbm.at[part], raw.at[part], load_sem.at[2 + i]))
    for copy in loads:
        copy.start()

    barrier = pltpu.get_barrier_semaphore()
    for d in range(1, TM):
        pl.semaphore_signal(barrier, inc=1, device_id={"tm": lax.rem(z + d, TM)}, device_id_type=MESH)
    for dy, dx in ((0, 1), (0, -1), (1, 0), (-1, 0)):
        pl.semaphore_signal(barrier, inc=1, device_id={"chan": chan_of(y + dy, x + dx, core)}, device_id_type=MESH)
    pl.semaphore_signal(barrier, inc=1, device_id={"chan": sibling}, device_id_type=MESH)

    def piece(p):
        return raw[pl.ds(p * HOP, HOP), :].astype(F32)

    for copy in loads[:3]:
        copy.wait()
    rising = taper[...]
    falling = 1.0 - rising
    halo_out[...] = jnp.dot(
        table[2 * SPAN :, :], (piece(0) * falling).astype(BF16), preferred_element_type=F32
    )
    pl.semaphore_wait(barrier, TM - 1 + 5)
    halo = pltpu.make_async_remote_copy(
        src_ref=halo_out, dst_ref=halo_in, send_sem=halo_sem.at[0], recv_sem=halo_sem.at[1],
        device_id={"tm": lax.rem(z + TM - 1, TM)}, device_id_type=MESH,
    )
    halo.start()

    waited = 1
    for pair in range(PIECES // 2):
        a, b = 2 * pair, 2 * pair + 1
        while waited < len(chunks) and b >= chunks[waited][0]:
            loads[2 + waited].wait()
            waited += 1
        one, two = piece(a), piece(b)
        up = jnp.concatenate([one * taper[...], two * taper[...]], axis=1).astype(BF16)
        first = jnp.dot(table[: 2 * SPAN, :], up, preferred_element_type=F32)
        spec[a] = first[:, :CH]
        spec[b] = first[:, CH:]
        fall = 1.0 - taper[...]
        down = jnp.concatenate([one * fall, two * fall], axis=1).astype(BF16)
        second = jnp.dot(table[2 * SPAN :, :], down, preferred_element_type=F32)
        if a > 0:
            spec[a - 1] = spec[a - 1] + second[:, :CH]
        spec[b - 1] = spec[b - 1] + second[:, CH:]

    def keep(k, spectra):
        real, imag = whiten(spectra)
        white[pl.ds(2 * k * SPAN, SPAN), :] = real
        white[pl.ds((2 * k + 1) * SPAN, SPAN), :] = imag

    for k in range(PIECES - 1):
        keep(k, spec[k])
    halo.wait_recv()
    keep(PIECES - 1, spec[PIECES - 1] + jnp.where(z == TM - 1, 0.0, halo_in[...]))

    order = (4, 3, 5, 2, 6, 1, 7)
    exchanges = []
    for h in range(2):
        for owner in range(TM):
            rows = [
                white[pl.ds(SMOOTH + owner * GROUP + h * BATCH + b, ROWS, stride=SPAN), :]
                for b in range(BATCH)
            ]
            to_tm[owner, h] = jnp.concatenate(rows, axis=0).astype(BF16)
        for i, d in enumerate(order):
            target = lax.rem(z + d, TM)
            copy = pltpu.make_async_remote_copy(
                src_ref=to_tm.at[target, h], dst_ref=from_tm.at[z, h],
                send_sem=tm_send.at[h, i], recv_sem=tm_recv.at[h, i],
                device_id={"tm": target}, device_id_type=MESH,
            )
            copy.start()
            exchanges.append(copy)
        from_tm[z, h] = to_tm[z, h]

    def unit(b, dp, dq, half=None):
        dy, dx = (dq, dp) if b % 2 == 0 else (dp, dq)
        ref = gathered.at[b, core, place_of(dy, dx)]
        return ref if half is None else ref.at[pl.ds(half * (DEPTH // 2), DEPTH // 2)]

    def neighbour(b, axis, sign):
        along_x = (axis == "p") == (b % 2 == 0)
        return chan_of(y, x + sign, core) if along_x else chan_of(y + sign, x, core)

    slots = {}
    for axis, sign in (("p", -1), ("p", 1)):
        for kind in ("whole", "half"):
            slots[(axis, sign, 0, kind)] = len(slots)
    for sign in (-1, 1):
        for dp in (0, -1, 1, 2):
            for kind in ("whole", "half"):
                slots[("q", sign, dp, kind)] = len(slots)

    def hand(b, dp, dq, axis, sign, half=None):
        kind = "whole" if half is None else "half"
        slot = slots[(axis, -sign, dp if axis == "q" else 0, kind)]
        ref = unit(b, dp, dq, half)
        pltpu.make_async_remote_copy(
            src_ref=ref, dst_ref=ref, send_sem=ici_send.at[b], recv_sem=ici_recv.at[b, slot],
            device_id={"chan": neighbour(b, axis, sign)}, device_id_type=MESH,
        ).start()

    def arrive(b, dp, dq, axis, side, half=None):
        kind = "whole" if half is None else "half"
        slot = slots[(axis, side, dp if axis == "q" else 0, kind)]
        ref = unit(b, dp, dq, half)
        pltpu.make_async_remote_copy(
            src_ref=ref, dst_ref=ref, send_sem=ici_send.at[b], recv_sem=ici_recv.at[b, slot],
            device_id={"chan": neighbour(b, axis, side)}, device_id_type=MESH,
        ).wait_recv()

    def share(b, dp, dq):
        ref = unit(b, dp, dq)
        pltpu.make_async_remote_copy(
            src_ref=ref, dst_ref=ref, send_sem=sib_send.at[b], recv_sem=sib_recv.at[b],
            device_id={"chan": sibling}, device_id_type=MESH,
        ).start()

    def own(b):
        for axis in ("p", "q"):
            for sign in (1, -1):
                hand(b, 0, 0, axis, sign)
        share(b, 0, 0)

    def first_p(b, side):
        arrive(b, side, 0, "p", side)
        hand(b, side, 0, "p", -side, half=0 if side < 0 else 1)
        hand(b, side, 0, "q", 1)
        hand(b, side, 0, "q", -1)
        share(b, side, 0)

    def second_p(b):
        arrive(b, 2, 0, "p", -1, half=0)
        arrive(b, 2, 0, "p", 1, half=1)
        hand(b, 2, 0, "q", 1)
        hand(b, 2, 0, "q", -1)
        share(b, 2, 0)

    def first_q(b, dp, side):
        arrive(b, dp, side, "q", side)
        hand(b, dp, side, "q", -side, half=0 if side < 0 else 1)
        share(b, dp, side)

    def second_q(b, dp):
        arrive(b, dp, 2, "q", -1, half=0)
        arrive(b, dp, 2, "q", 1, half=1)
        share(b, dp, 2)

    for h in range(2):
        for copy in exchanges[h * (TM - 1) : (h + 1) * (TM - 1)]:
            copy.wait_recv()
        parts = [from_tm[s, h].astype(F32) for s in range(TM)]
        for b in range(BATCH):
            whole = jnp.concatenate([part[b * ROWS : (b + 1) * ROWS] for part in parts], axis=0)
            gathered[h * BATCH + b, core, place] = whole.astype(BF16)
        for b in range(BATCH):
            own(h * BATCH + b)

    for pair in ((0, 1), (2, 3)):
        for side in (-1, 1):
            for b in pair:
                first_p(b, side)
    for pair in ((0, 1), (2, 3)):
        for side in (-1, 1):
            for b in pair:
                first_q(b, 0, side)
        for b in pair:
            second_p(b)

    parity = lax.rem(lax.broadcasted_iota(jnp.int32, (DEPTH, CH), 0), 2)
    for b in range(GROUP):
        rows = gathered[b, core, place].astype(F32)
        turned = jnp.where(parity == 0, pltpu.roll(rows, DEPTH - 1, 0), -pltpu.roll(rows, 1, 0))
        own_t[b, :CH, :] = rows.T.astype(BF16)
        own_t[b, CH:, :] = turned.T.astype(BF16)

    for pair in ((0, 1), (2, 3)):
        for dp in (-1, 1):
            for side in (-1, 1):
                for b in pair:
                    first_q(b, dp, side)
        for b in pair:
            second_q(b, 0)
    for pair in ((0, 1), (2, 3)):
        for side in (-1, 1):
            for b in pair:
                first_q(b, 2, side)
    for pair in ((0, 1), (2, 3)):
        for dp in (-1, 1):
            for b in pair:
                second_q(b, dp)
    for pair in ((0, 1), (2, 3)):
        for b in pair:
            second_q(b, 2)

    halo.wait_send()
    for copy in exchanges:
        copy.wait_send()
    for b in range(GROUP):
        sent = gathered.at[b, core, pl.ds(0, SIDE * SIDE - 1)]
        pltpu.make_async_remote_copy(
            src_ref=sent, dst_ref=sent, send_sem=ici_send.at[b], recv_sem=ici_recv.at[b, 0],
            device_id={"chan": sibling}, device_id_type=MESH,
        ).wait_send()
        shared = pltpu.make_async_remote_copy(
            src_ref=gathered.at[b, core], dst_ref=gathered.at[b, 1 - core],
            send_sem=sib_send.at[b], recv_sem=sib_recv.at[b],
            device_id={"chan": sibling}, device_id_type=MESH,
        )
        shared.wait_send()
        shared.wait_recv()


TILE = 4


def product_kernel(gathered, own_t, out, held, sems):
    steps = SIDE * SIDE // TILE
    wide = TILE * CORES * CH

    def copy_of(t):
        b, g = t // steps, lax.rem(t, steps)
        columns = pl.ds(pl.multiple_of(g * wide, wide), wide)
        return pltpu.make_async_copy(held.at[b, :, :, columns], out.at[b, :, :, columns], sems.at[t])

    def step(t, carry):
        b, g = t // steps, lax.rem(t, steps)
        for i in range(TILE):
            q = g * TILE + i
            right = jnp.concatenate([gathered[b, 0, q], gathered[b, 1, q]], axis=1)
            product = jnp.dot(own_t[b], right, preferred_element_type=F32) * (1.0 / FRAMES)
            product = product.astype(BF16)
            columns = pl.ds(pl.multiple_of(q * CORES * CH, CORES * CH), CORES * CH)
            held[b, 0, :, columns] = product[:CH]
            held[b, 1, :, columns] = product[CH:]
        copy_of(t).start()
        return carry

    lax.fori_loop(0, GROUP * steps, step, 0)

    def finish(t, carry):
        copy_of(t).wait()
        return carry

    lax.fori_loop(0, GROUP * steps, finish, 0)


def local(raw_traces):
    any_space = pl.BlockSpec(memory_space=pl.ANY)
    vmem = pl.BlockSpec(memory_space=pltpu.VMEM)
    gathered, own_t = pl.pallas_call(
        gather_kernel,
        out_shape=(
            pltpu.VMEM((GROUP, CORES, SIDE * SIDE, DEPTH, CH), BF16),
            pltpu.VMEM((GROUP, 2 * CH, DEPTH), BF16),
        ),
        in_specs=[any_space] * 3,
        out_specs=(vmem, vmem),
        scratch_shapes=[
            pltpu.VMEM((PIECES * HOP, CH), BF16),
            pltpu.VMEM((4 * SPAN, HOP), BF16),
            pltpu.VMEM((HOP, CH), F32),
            pltpu.VMEM((PIECES, 2 * SPAN, CH), F32),
            pltpu.VMEM((2 * SPAN, CH), F32),
            pltpu.VMEM((2 * SPAN, CH), F32),
            pltpu.VMEM((ROWS * SPAN, CH), F32),
            pltpu.VMEM((TM, 2, BATCH * ROWS, CH), BF16),
            pltpu.VMEM((TM, 2, BATCH * ROWS, CH), BF16),
            pltpu.SemaphoreType.DMA((6,)),
            pltpu.SemaphoreType.DMA((2,)),
            pltpu.SemaphoreType.DMA((2, TM - 1)),
            pltpu.SemaphoreType.DMA((2, TM - 1)),
            pltpu.SemaphoreType.DMA((GROUP,)),
            pltpu.SemaphoreType.DMA((GROUP, 20)),
            pltpu.SemaphoreType.DMA((GROUP,)),
            pltpu.SemaphoreType.DMA((GROUP,)),
        ],
        compiler_params=pltpu.CompilerParams(
            collective_id=0, has_side_effects=True, vmem_limit_bytes=24 * 1024 * 1024
        ),
    )(raw_traces, jnp.asarray(spectral_table()), jnp.asarray(taper_half()))
    return pl.pallas_call(
        product_kernel,
        out_shape=jax.ShapeDtypeStruct((GROUP, 2, CH, SIDE * SIDE * CORES * CH), BF16),
        in_specs=[vmem, vmem],
        out_specs=any_space,
        scratch_shapes=[
            pltpu.VMEM((GROUP, 2, CH, SIDE * SIDE * CORES * CH), BF16),
            pltpu.SemaphoreType.DMA((GROUP * SIDE * SIDE // TILE,)),
        ],
        compiler_params=pltpu.CompilerParams(vmem_limit_bytes=24 * 1024 * 1024),
    )(
        pltpu.with_memory_space_constraint(gathered, pltpu.VMEM),
        pltpu.with_memory_space_constraint(own_t, pltpu.VMEM),
    )


def solution(mesh):
    return jax.shard_map(
        local, mesh=mesh, in_specs=(P("tm", "chan"),), out_specs=P("tm", None, "chan", None), check_vma=False
    )
```

time: 307 us -> 49.5 us (0.16)
  waiting for transfers between devices: 211 us -> 0 us
  local copies, waits for them, and re-layouts: 51.9 us -> 3.27 us
  Pallas kernels: 0 us -> 46.1 us
  matrix products: 13.8 us -> 0 us
  between operations: 13.5 us -> 0.01 us
  other arithmetic: 8.71 us -> 0 us
  starting transfers between devices: 8.03 us -> 0 us
    all_to_all x1 -> x0, waiting for transfers between devices: 142 us -> none  [local(): lax.all_to_all(everyone, 'tm', split_axis=2, concat_axis=0, tiled=True)]
    all_gather x1 -> x0, waiting for transfers between devices: 64.1 us -> none  [local(): everyone = lax.all_gather(whitened, 'chan', axis=3, tiled=True)]
    pallas_call x0 -> x2, Pallas kernels: none -> 46.1 us  [the longest x1 40.1 us: local(): pl.pallas_call(gather_kernel, out_shape=(pltpu.VMEM((GROUP, CORES, SIDE *...]
    all_to_all x1 -> x0, local copies, waits for them, and re-layouts: 15.6 us -> none  [local(): lax.all_to_all(everyone, 'tm', split_axis=2, concat_axis=0, tiled=True)]
    dot_general x2 -> x0, matrix products: 13.8 us -> none  [the longest x1 11.1 us: cross_block(): jnp.einsum('kpgr,kpgoc->gorc', own_rows, partner, preferred_element_type=...]
    all_gather x1 -> x0, local copies, waits for them, and re-layouts: 12.7 us -> none  [local(): everyone = lax.all_gather(whitened, 'chan', axis=3, tiled=True)]
    convert_element_type x1 -> x0, local copies, waits for them, and re-layouts: 12 us -> none  [cross_block(): return (products / frames_all).astype(jnp.bfloat16)]
    all_to_all x1 -> x0, starting transfers between devices: 6.73 us -> none  [local(): lax.all_to_all(everyone, 'tm', split_axis=2, concat_axis=0, tiled=True)]
  transfers between devices with their start and end apart: 3 -> 0, of which waited for: 3 -> 0; matrix products, arithmetic and copies ran while one was open for 0% -> 0% of each run, Pallas kernels for 0% -> 0%
where the time goes in v1:
time: 49.5 us; the launch traced here: 49.4 us
  Pallas kernels  46.1 us (93%)
  local copies, waits for them, and re-layouts  3.27 us (7%)
    pallas_call x1, Pallas kernels, local(): pl.pallas_call(gather_kernel, out_shape=(pltpu.VMEM((GROUP, CORES, SIDE *...  40.1 us
    pallas_call x1, Pallas kernels, local(): pl.pallas_call(product_kernel, out_shape=jax.ShapeDtypeStruct((GROUP, 2,...  6.01 us
    unnamed x6, local copies, waits for them, and re-layouts  3.27 us

profile of v1, /device:TPU:1, one launch (start us, length us, event | category | flops | bytes accessed | tf_op | source)
XLA Modules:
  0.0 49.4 jit_solution(7137701430169552599)
XLA Ops:
  0.0 0.0 copy-start
  0.0 1.4 %copy-done = bf16[6144,128]{1,0:T(8,128)(2,1)S(1)} copy-done((bf16[6144,128]{1,0:T(8,128)(2,1)S(1)}, bf16[6144,128]{1,0:T(8,128)(2,1)}, u32[]{:S(2)}) %copy-start) | copy-done | bytes 1572888
  1.4 0.0 copy-start.1
  1.4 0.9 %copy-done.1 = f32[512,128]{1,0:T(8,128)S(1)} copy-done((f32[512,128]{1,0:T(8,128)S(1)}, f32[512,128]{1,0:T(8,128)}, u32[]{:S(2)}) %copy-start.1) | copy-done | bytes 262168
  2.4 0.0 copy-start.2
  2.4 0.9 %copy-done.2 = bf16[160,512]{1,0:T(8,128)(2,1)S(1)} copy-done((bf16[160,512]{1,0:T(8,128)(2,1)S(1)}, bf16[160,512]{1,0:T(8,128)(2,1)}, u32[]{:S(2)}) %copy-start.2) | copy-done | bytes 163864
  3.3 40.1 %shard_map.37 = (bf16[4,2,16,192,128]{4,3,2,1,0:T(8,128)(2,1)S(1)}, bf16[4,256,192]{2,1,0:T(8,128)(2,1)S(1)}) custom-call(bf16[6144,128]{1,0:T(8,128)(2,1)S(1)} %copy-done, bf16[160,512]{1,0:T(8,128)(2,1)S(1)} %copy-done.2, f32[512,128]{1,0:T(8,128)S(1)} %copy-done.1), custom_call_target="tpu_custom_call" | custom-call | tf_op jit(solution)/shard_map/pallas_call | solution.py:338
  43.3 6.0 %shard_map.38 = bf16[4,2,128,4096]{3,2,1,0:T(8,128)(2,1)} custom-call(bf16[4,2,16,192,128]{4,3,2,1,0:T(8,128)(2,1)S(1)} %get-tuple-element.7.gathered, bf16[4,256,192]{2,1,0:T(8,128)(2,1)S(1)} %get-tuple-element.8.own_t), custom_call_target="tpu_custom_call" | custom-call | tf_op jit(solution)/shard_map/pallas_call | solution.py:369
Async XLA Ops:
  0.0 1.4 %copy-start = (bf16[6144,128]{1,0:T(8,128)(2,1)S(1)}, bf16[6144,128]{1,0:T(8,128)(2,1)}, u32[]{:S(2)}) copy-start(bf16[6144,128]{1,0:T(8,128)(2,1)} %raw_hbm.1) | copy-start | bytes 4718596
  1.4 0.9 %copy-start.1 = (f32[512,128]{1,0:T(8,128)S(1)}, f32[512,128]{1,0:T(8,128)}, u32[]{:S(2)}) copy-start(f32[512,128]{1,0:T(8,128)} %constant.5.clone.taper_hbm) | copy-start | bytes 786436
  2.4 0.9 %copy-start.2 = (bf16[160,512]{1,0:T(8,128)(2,1)S(1)}, bf16[160,512]{1,0:T(8,128)(2,1)}, u32[]{:S(2)}) copy-start(bf16[160,512]{1,0:T(8,128)(2,1)} %constant.4.clone.table_hbm) | copy-start | bytes 491524

commit v2 on v1

v2 whole, which is shorter than its diff:
```python
import functools
import math

import jax
import jax.numpy as jnp
import numpy as np
from jax import lax
from jax.experimental import pallas as pl
from jax.experimental.pallas import tpu as pltpu
from jax.sharding import PartitionSpec as P

NFFT = 1024
HOP = NFFT // 2
NBINS = 32
SMOOTH = 4
BAND_START = 64
SPAN = NBINS + 2 * SMOOTH
FLOOR = 0.125 * math.sqrt(NFFT)
TM = 8
SIDE = 4
CORES = 2
CH = 128
PIECES = 12
FRAMES = TM * PIECES
GROUP = NBINS // TM
ROWS = 2 * PIECES
PAIR = 2 * ROWS
SIZES = (PAIR, 2 * PAIR, 2 * PAIR, 2 * PAIR, PAIR)
STARTS = (0, PAIR, 3 * PAIR, 5 * PAIR, 7 * PAIR)
UNIT = 8 * PAIR
CUTS = (32, PAIR, PAIR, PAIR, 16)
DEPTH = 5 * PAIR
MESH = pl.DeviceIdType.MESH
F32 = jnp.float32
BF16 = jnp.bfloat16


def spectral_table():
    sample = np.arange(NFFT)
    bins = BAND_START - SMOOTH + np.arange(SPAN)
    angles = (sample[:, None] * bins[None, :] % NFFT).astype(np.float64) * (2.0 * math.pi / NFFT)
    table = np.concatenate([np.cos(angles), -np.sin(angles)], axis=1).astype(np.float32)
    halves = np.concatenate([table[:HOP].T, table[HOP:].T], axis=0)
    return jnp.asarray(halves.astype(BF16))


def taper_half():
    sample = np.arange(HOP, dtype=np.float64)
    half = 0.5 - 0.5 * np.cos(sample * (2.0 * math.pi / NFFT))
    return jnp.asarray(np.broadcast_to(half.astype(np.float32)[:, None], (HOP, CH)))


def part_of(c, half=None):
    if half is None:
        return pl.ds(STARTS[c], SIZES[c])
    if half == 0:
        return pl.ds(STARTS[c], CUTS[c])
    return pl.ds(STARTS[c] + CUTS[c], SIZES[c] - CUTS[c])


def depth_of(i):
    starts = [STARTS[0]] + [STARTS[c] + i * PAIR for c in (1, 2, 3)] + [STARTS[4]]
    return [pl.ds(start, PAIR) for start in starts]


def whiten(spectra):
    real, imag = spectra[:SPAN], spectra[SPAN:]
    magnitude = jnp.sqrt(real * real + imag * imag)
    two = magnitude + pltpu.roll(magnitude, SPAN - 1, 0)
    four = two + pltpu.roll(two, SPAN - 2, 0)
    eight = four + pltpu.roll(four, SPAN - 4, 0)
    nine = eight + pltpu.roll(magnitude, SPAN - 8, 0)
    factor = 1.0 / jnp.maximum(nine * (1.0 / (2 * SMOOTH + 1)), FLOOR)
    factor = pltpu.roll(factor, SMOOTH, 0)
    return real * factor, imag * factor


def gather_kernel(
    raw_hbm, table_hbm, taper_hbm, gathered, own_t,
    raw, table, taper, spec, halo_out, halo_in, white, to_tm, from_tm,
    load_sem, halo_sem, tm_send, tm_recv, ici_send, ici_recv, sib_send, sib_recv,
):
    z = lax.axis_index("tm")
    chan = lax.axis_index("chan")
    core = lax.rem(chan, CORES)
    place = chan // CORES
    y, x = place // SIDE, lax.rem(place, SIDE)

    def chan_of(yy, xx, cc):
        return (lax.rem(yy + SIDE, SIDE) * SIDE + lax.rem(xx + SIDE, SIDE)) * CORES + cc

    sibling = chan_of(y, x, 1 - core)

    chunks = [(0, 1), (1, 3), (4, 4), (8, 4)]
    loads = [
        pltpu.make_async_copy(table_hbm, table, load_sem.at[0]),
        pltpu.make_async_copy(taper_hbm, taper, load_sem.at[1]),
    ]
    for i, (first, count) in enumerate(chunks):
        part = pl.ds(first * HOP, count * HOP)
        loads.append(pltpu.make_async_copy(raw_hbm.at[part], raw.at[part], load_sem.at[2 + i]))
    for copy in loads:
        copy.start()

    barrier = pltpu.get_barrier_semaphore()
    for d in range(1, TM):
        pl.semaphore_signal(barrier, inc=1, device_id={"tm": lax.rem(z + d, TM)}, device_id_type=MESH)
    for dy, dx in ((0, 1), (0, -1), (1, 0), (-1, 0)):
        pl.semaphore_signal(barrier, inc=1, device_id={"chan": chan_of(y + dy, x + dx, core)}, device_id_type=MESH)
    pl.semaphore_signal(barrier, inc=1, device_id={"chan": sibling}, device_id_type=MESH)

    def piece(p):
        return raw[pl.ds(p * HOP, HOP), :].astype(F32)

    for copy in loads[:3]:
        copy.wait()
    rising = taper[...]
    falling = 1.0 - rising
    halo_out[...] = jnp.dot(
        table[2 * SPAN :, :], (piece(0) * falling).astype(BF16), preferred_element_type=F32
    )
    pl.semaphore_wait(barrier, TM - 1 + 5)
    halo = pltpu.make_async_remote_copy(
        src_ref=halo_out, dst_ref=halo_in, send_sem=halo_sem.at[0], recv_sem=halo_sem.at[1],
        device_id={"tm": lax.rem(z + TM - 1, TM)}, device_id_type=MESH,
    )
    halo.start()

    waited = 1
    for pair in range(PIECES // 2):
        a, b = 2 * pair, 2 * pair + 1
        while waited < len(chunks) and b >= chunks[waited][0]:
            loads[2 + waited].wait()
            waited += 1
        one, two = piece(a), piece(b)
        up = jnp.concatenate([one * taper[...], two * taper[...]], axis=1).astype(BF16)
        first = jnp.dot(table[: 2 * SPAN, :], up, preferred_element_type=F32)
        spec[a] = first[:, :CH]
        spec[b] = first[:, CH:]
        fall = 1.0 - taper[...]
        down = jnp.concatenate([one * fall, two * fall], axis=1).astype(BF16)
        second = jnp.dot(table[2 * SPAN :, :], down, preferred_element_type=F32)
        if a > 0:
            spec[a - 1] = spec[a - 1] + second[:, :CH]
        spec[b - 1] = spec[b - 1] + second[:, CH:]

    def keep(k, spectra):
        real, imag = whiten(spectra)
        white[pl.ds(2 * k * SPAN, SPAN), :] = real
        white[pl.ds((2 * k + 1) * SPAN, SPAN), :] = imag

    for k in range(PIECES - 1):
        keep(k, spec[k])
    halo.wait_recv()
    keep(PIECES - 1, spec[PIECES - 1] + jnp.where(z == TM - 1, 0.0, halo_in[...]))

    def group_rows(owner):
        rows = [
            white[pl.ds(SMOOTH + owner * GROUP + b, ROWS, stride=SPAN), :] for b in range(GROUP)
        ]
        return jnp.concatenate(rows, axis=0)

    def lines(dp, dq, m):
        dy, dx = (dq, dp) if m == 0 else (dp, dq)
        return lax.rem(y + dy + SIDE, SIDE), lax.rem(x + dx + SIDE, SIDE)

    def unit(m, c, dp, half=None):
        yy, xx = lines(dp, 0, m)
        return gathered.at[m, core, yy, xx, part_of(c, half)]

    def line(m, c, dq, half=None):
        yy, xx = lines(0, dq, m)
        if m == 0:
            return gathered.at[m, core, yy, :, part_of(c, half)]
        return gathered.at[m, core, :, xx, part_of(c, half)]

    def neighbour(m, axis, sign):
        along_x = (axis == 0) == (m == 0)
        return chan_of(y, x + sign, core) if along_x else chan_of(y + sign, x, core)

    def copy_of(m, c, axis, side, half, ref, to):
        slot = axis * 4 + (0 if side < 0 else 1) * 2 + (0 if half is None else 1)
        return pltpu.make_async_remote_copy(
            src_ref=ref, dst_ref=ref, send_sem=ici_send.at[m, axis], recv_sem=ici_recv.at[m, c, slot],
            device_id={"chan": neighbour(m, axis, to)}, device_id_type=MESH,
        )

    def hand(m, c, axis, sign, ref, half=None):
        copy_of(m, c, axis, -sign, half, ref, sign).start()

    def arrive(m, c, axis, side, ref, half=None):
        copy_of(m, c, axis, side, half, ref, side).wait_recv()

    def share(m, c, dq):
        ref = line(m, c, dq)
        pltpu.make_async_remote_copy(
            src_ref=ref, dst_ref=ref, send_sem=sib_send.at[m], recv_sem=sib_recv.at[m],
            device_id={"chan": sibling}, device_id_type=MESH,
        ).start()

    def own(c):
        for m in range(2):
            for sign in (1, -1):
                hand(m, c, 0, sign, unit(m, c, 0))

    def first(c):
        for side in (-1, 1):
            for m in range(2):
                arrive(m, c, 0, side, unit(m, c, side))
                half = 0 if side < 0 else 1
                hand(m, c, 0, -side, unit(m, c, side, half), half)

    def second(c):
        for m in range(2):
            arrive(m, c, 0, -1, unit(m, c, 2, 0), 0)
            arrive(m, c, 0, 1, unit(m, c, 2, 1), 1)
            hand(m, c, 1, 1, line(m, c, 0))
            hand(m, c, 1, -1, line(m, c, 0))
            share(m, c, 0)

    def third(c):
        for side in (-1, 1):
            for m in range(2):
                arrive(m, c, 1, side, line(m, c, side))
                half = 0 if side < 0 else 1
                hand(m, c, 1, -side, line(m, c, side, half), half)
                share(m, c, side)

    def fourth(c):
        for m in range(2):
            arrive(m, c, 1, -1, line(m, c, 2, 0), 0)
            arrive(m, c, 1, 1, line(m, c, 2, 1), 1)
            share(m, c, 2)

    def keep_unit(c, m, rows):
        gathered[m, core, y, x, pl.ds(STARTS[c], SIZES[c]), :] = rows.astype(BF16)

    order = (1, -1, 2, -2, 3, -3, 4)
    own_rows = group_rows(z)
    for m in range(2):
        keep_unit(0, m, own_rows[m * PAIR : (m + 1) * PAIR])
    own(0)
    exchanges = {}
    for i, d in enumerate(order):
        target = lax.rem(z + d + TM, TM)
        to_tm[i] = group_rows(target).astype(BF16)
        exchanges[d] = pltpu.make_async_remote_copy(
            src_ref=to_tm.at[i], dst_ref=from_tm.at[i],
            send_sem=tm_send.at[i], recv_sem=tm_recv.at[i],
            device_id={"tm": target}, device_id_type=MESH,
        )
        exchanges[d].start()

    def receive(c):
        if c == 4:
            exchanges[4].wait_recv()
            rows = from_tm[order.index(4)]
            for m in range(2):
                keep_unit(c, m, rows[m * PAIR : (m + 1) * PAIR])
        else:
            both = []
            for d in (c, -c):
                exchanges[d].wait_recv()
                both.append(from_tm[order.index(d)].astype(F32))
            for m in range(2):
                parts = []
                for b in range(2):
                    start = (2 * m + b) * ROWS
                    parts += [rows[start : start + ROWS] for rows in both]
                keep_unit(c, m, jnp.concatenate(parts, axis=0))
        own(c)

    def transpose_own():
        row = lax.broadcasted_iota(jnp.int32, (DEPTH, CH), 0)
        for b in range(GROUP):
            m, i = b // 2, b % 2
            rows = jnp.concatenate([gathered[m, core, y, x, part, :] for part in depth_of(i)], axis=0).astype(F32)
            other = (1 - i) * ROWS
            kept = True
            for start in (0, DEPTH - PAIR):
                kept = kept & ((row < start + other) | (row >= start + other + ROWS))
            rows = jnp.where(kept, rows, 0.0)
            turned = jnp.where(lax.rem(row, 2) == 0, pltpu.roll(rows, DEPTH - 1, 0), -pltpu.roll(rows, 1, 0))
            own_t[b, :CH, :] = rows.T.astype(BF16)
            own_t[b, CH:, :] = turned.T.astype(BF16)

    receive(1)
    first(0)
    second(0)
    receive(2)
    first(1)
    second(1)
    third(0)
    receive(3)
    first(2)
    fourth(0)
    second(2)
    third(1)
    receive(4)
    first(3)
    second(3)
    transpose_own()
    fourth(1)
    third(2)
    first(4)
    second(4)
    fourth(2)
    third(3)
    fourth(3)
    third(4)
    fourth(4)

    halo.wait_send()
    for d in order:
        exchanges[d].wait_send()
    for m in range(2):
        for axis, sent in ((0, gathered.at[m, core, 0, pl.ds(0, 3)]), (1, gathered.at[m, core, pl.ds(0, 3)])):
            pltpu.make_async_remote_copy(
                src_ref=sent, dst_ref=sent, send_sem=ici_send.at[m, axis], recv_sem=ici_recv.at[m, 0, 0],
                device_id={"chan": sibling}, device_id_type=MESH,
            ).wait_send()
        shared = pltpu.make_async_remote_copy(
            src_ref=gathered.at[m, core], dst_ref=gathered.at[m, 1 - core],
            send_sem=sib_send.at[m], recv_sem=sib_recv.at[m],
            device_id={"chan": sibling}, device_id_type=MESH,
        )
        shared.wait_send()
        shared.wait_recv()


TILE = 4


def product_kernel(gathered, own_t, out, held, sems):
    steps = SIDE * SIDE // TILE
    wide = TILE * CORES * CH

    def copy_of(b, g):
        columns = pl.ds(pl.multiple_of(g * wide, wide), wide)
        return pltpu.make_async_copy(held.at[b, :, :, columns], out.at[b, :, :, columns], sems.at[b, g])

    def step(g, b):
        m, i = b // 2, b % 2
        for x in range(SIDE):
            right = jnp.concatenate(
                [jnp.concatenate([gathered[m, c, g, x, part, :] for part in depth_of(i)], axis=0) for c in range(CORES)],
                axis=1,
            )
            product = jnp.dot(own_t[b], right, preferred_element_type=F32) * (1.0 / FRAMES)
            product = product.astype(BF16)
            columns = pl.ds(pl.multiple_of(g * wide + x * CORES * CH, CORES * CH), CORES * CH)
            held[b, 0, :, columns] = product[:CH]
            held[b, 1, :, columns] = product[CH:]
        copy_of(b, g).start()

    for b in range(GROUP):
        @pl.loop(0, steps)
        def _(g):
            step(g, b)

    for b in range(GROUP):
        @pl.loop(0, steps)
        def _(g):
            copy_of(b, g).wait()


def local(raw_traces):
    any_space = pl.BlockSpec(memory_space=pl.ANY)
    vmem = pl.BlockSpec(memory_space=pltpu.VMEM)
    gathered, own_t = pl.pallas_call(
        gather_kernel,
        out_shape=(
            pltpu.VMEM((2, CORES, SIDE, SIDE, UNIT, CH), BF16),
            pltpu.VMEM((GROUP, 2 * CH, DEPTH), BF16),
        ),
        in_specs=[any_space] * 3,
        out_specs=(vmem, vmem),
        scratch_shapes=[
            pltpu.VMEM((PIECES * HOP, CH), BF16),
            pltpu.VMEM((4 * SPAN, HOP), BF16),
            pltpu.VMEM((HOP, CH), F32),
            pltpu.VMEM((PIECES, 2 * SPAN, CH), F32),
            pltpu.VMEM((2 * SPAN, CH), F32),
            pltpu.VMEM((2 * SPAN, CH), F32),
            pltpu.VMEM((ROWS * SPAN, CH), F32),
            pltpu.VMEM((TM - 1, GROUP * ROWS, CH), BF16),
            pltpu.VMEM((TM - 1, GROUP * ROWS, CH), BF16),
            pltpu.SemaphoreType.DMA((6,)),
            pltpu.SemaphoreType.DMA((2,)),
            pltpu.SemaphoreType.DMA((TM - 1,)),
            pltpu.SemaphoreType.DMA((TM - 1,)),
            pltpu.SemaphoreType.DMA((2, 2)),
            pltpu.SemaphoreType.DMA((2, 5, 8)),
            pltpu.SemaphoreType.DMA((2,)),
            pltpu.SemaphoreType.DMA((2,)),
        ],
        compiler_params=pltpu.CompilerParams(
            collective_id=0, has_side_effects=True, vmem_limit_bytes=24 * 1024 * 1024
        ),
    )(*(pltpu.with_memory_space_constraint(a, pltpu.HBM) for a in (raw_traces, spectral_table(), taper_half())))
    return pl.pallas_call(
        product_kernel,
        out_shape=jax.ShapeDtypeStruct((GROUP, 2, CH, SIDE * SIDE * CORES * CH), BF16),
        in_specs=[vmem, vmem],
        out_specs=any_space,
        scratch_shapes=[
            pltpu.VMEM((GROUP, 2, CH, SIDE * SIDE * CORES * CH), BF16),
            pltpu.SemaphoreType.DMA((GROUP, SIDE * SIDE // TILE)),
        ],
        compiler_params=pltpu.CompilerParams(vmem_limit_bytes=24 * 1024 * 1024),
    )(
        pltpu.with_memory_space_constraint(gathered, pltpu.VMEM),
        pltpu.with_memory_space_constraint(own_t, pltpu.VMEM),
    )


def solution(mesh):
    return jax.shard_map(
        local, mesh=mesh, in_specs=(P("tm", "chan"),), out_specs=P("tm", None, "chan", None), check_vma=False
    )
```

time: 49.5 us -> 62.4 us (1.26)
  Pallas kernels: 46.1 us -> 60.7 us
  local copies, waits for them, and re-layouts: 3.27 us -> 1.52 us
    pallas_call x1, Pallas kernels: 40.1 us -> 54.6 us  [local(): pl.pallas_call(gather_kernel, out_shape=(pltpu.VMEM((2, CORES, SIDE, SIDE...]
    unnamed x6 -> x0, local copies, waits for them, and re-layouts: 3.27 us -> none
    another operation x0 -> x1, local copies, waits for them, and re-layouts: none -> 1.52 us
where the time goes in v2:
time: 62.4 us; the launch traced here: 62.3 us
  Pallas kernels  60.7 us (97%)
  local copies, waits for them, and re-layouts  1.52 us (2%)
    pallas_call x1, Pallas kernels, local(): pl.pallas_call(gather_kernel, out_shape=(pltpu.VMEM((2, CORES, SIDE, SIDE...  54.6 us
    pallas_call x1, Pallas kernels, local(): pl.pallas_call(product_kernel, out_shape=jax.ShapeDtypeStruct((GROUP, 2,...  6.09 us
    another operation x1, local copies, waits for them, and re-layouts  1.52 us

profile of v2, /device:TPU:1, one launch (start us, length us, event | category | flops | bytes accessed | tf_op | source)
XLA Modules:
  0.0 62.3 jit_solution(14688291267903810197)
XLA Ops:
  0.0 1.5 %jit_solution_.3.taper_hbm = f32[512,128]{1,0:T(8,128)} broadcast(f32[512]{0:T(512)} %constant.5.clone), dimensions={0} | broadcast | bytes 264192 | tf_op jit(solution)
  1.5 54.6 %shard_map.37 = (bf16[2,2,4,4,384,128]{5,4,3,2,1,0:T(8,128)(2,1)S(1)}, bf16[4,256,240]{2,1,0:T(8,128)(2,1)S(1)}) custom-call(bf16[6144,128]{1,0:T(8,128)(2,1)} %raw_hbm.1, bf16[160,512]{1,0:T(8,128)(2,1)} %constant.4.clone.table_hbm, f32[512,128]{1,0:T(8,128)} %jit_solution_.3.taper_hbm), custom_call_target="tpu_custom_call" | custom-call | tf_op jit(solution)/shard_map/pallas_call | solution.py:370
  56.2 6.1 %shard_map.38 = bf16[4,2,128,4096]{3,2,1,0:T(8,128)(2,1)} custom-call(bf16[2,2,4,4,384,128]{5,4,3,2,1,0:T(8,128)(2,1)S(1)} %get-tuple-element.7.gathered, bf16[4,256,240]{2,1,0:T(8,128)(2,1)S(1)} %get-tuple-element.8.own_t), custom_call_target="tpu_custom_call" | custom-call | tf_op jit(solution)/shard_map/pallas_call | solution.py:401

commit v3 on v2

v3 whole, which is shorter than its diff:
```python
import functools
import math

import jax
import jax.numpy as jnp
import numpy as np
from jax import lax
from jax.experimental import pallas as pl
from jax.experimental.pallas import tpu as pltpu
from jax.sharding import PartitionSpec as P

NFFT = 1024
HOP = NFFT // 2
NBINS = 32
SMOOTH = 4
BAND_START = 64
SPAN = NBINS + 2 * SMOOTH
FLOOR = 0.125 * math.sqrt(NFFT)
TM = 8
SIDE = 4
CORES = 2
CH = 128
PIECES = 12
FRAMES = TM * PIECES
GROUP = NBINS // TM
ROWS = 2 * PIECES
HALF = TM // 2
FULL = 2 * (PIECES - 1)
EARLY = 2 * HALF * FULL
LAST = 2 * 2 * TM
UNIT = 2 * EARLY + LAST
STARTS = (0, EARLY)
SIZES = (EARLY, EARLY + LAST)
CUT = 96
DEPTH = 2 * CUT + LAST // 2
MESH = pl.DeviceIdType.MESH
F32 = jnp.float32
BF16 = jnp.bfloat16


def spectral_table():
    sample = np.arange(NFFT)
    bins = BAND_START - SMOOTH + np.arange(SPAN)
    angles = (sample[:, None] * bins[None, :] % NFFT).astype(np.float64) * (2.0 * math.pi / NFFT)
    table = np.concatenate([np.cos(angles), -np.sin(angles)], axis=1).astype(np.float32)
    halves = np.concatenate([table[:HOP].T, table[HOP:].T], axis=0)
    return jnp.asarray(halves.astype(BF16))


def fill_taper(taper):
    step = 2.0 * math.pi / NFFT
    sample = lax.broadcasted_iota(jnp.int32, (8, CH), 0).astype(F32) * step
    cosine, sine = 0.5 * jnp.cos(sample), 0.5 * jnp.sin(sample)
    for i in range(HOP // 8):
        angle = 8 * i * step
        taper[8 * i : 8 * i + 8, :] = 0.5 - math.cos(angle) * cosine + math.sin(angle) * sine


def part_of(c, half=None):
    if half is None:
        return pl.ds(STARTS[c], SIZES[c])
    if half == 0:
        return pl.ds(STARTS[c], CUT)
    return pl.ds(STARTS[c] + CUT, SIZES[c] - CUT)


def depth_of(i):
    shift = i * (EARLY - CUT)
    return [pl.ds(shift, CUT), pl.ds(EARLY + shift, CUT), pl.ds(2 * EARLY + i * LAST // 2, LAST // 2)]


def whiten(spectra):
    real, imag = spectra[:SPAN], spectra[SPAN:]
    magnitude = jnp.sqrt(real * real + imag * imag)
    two = magnitude + pltpu.roll(magnitude, SPAN - 1, 0)
    four = two + pltpu.roll(two, SPAN - 2, 0)
    eight = four + pltpu.roll(four, SPAN - 4, 0)
    nine = eight + pltpu.roll(magnitude, SPAN - 8, 0)
    factor = 1.0 / jnp.maximum(nine * (1.0 / (2 * SMOOTH + 1)), FLOOR)
    factor = pltpu.roll(factor, SMOOTH, 0)
    return real * factor, imag * factor


def gather_kernel(
    raw_hbm, table_hbm, gathered, own_t,
    raw, table, taper, spec, halo_out, halo_in, white, to_tm, from_tm, to_last, from_last, last, stage,
    load_sem, halo_sem, tm_send, tm_recv, ici_send, ici_recv, sib_send, sib_recv,
):
    z = lax.axis_index("tm")
    chan = lax.axis_index("chan")
    core = lax.rem(chan, CORES)
    place = chan // CORES
    y, x = place // SIDE, lax.rem(place, SIDE)

    def chan_of(yy, xx, cc):
        return (lax.rem(yy + SIDE, SIDE) * SIDE + lax.rem(xx + SIDE, SIDE)) * CORES + cc

    sibling = chan_of(y, x, 1 - core)

    chunks = [(0, 1), (1, 3), (4, 4), (8, 4)]
    loads = [pltpu.make_async_copy(table_hbm, table, load_sem.at[0])]
    for i, (first, count) in enumerate(chunks):
        part = pl.ds(first * HOP, count * HOP)
        loads.append(pltpu.make_async_copy(raw_hbm.at[part], raw.at[part], load_sem.at[1 + i]))
    for copy in loads:
        copy.start()

    barrier = pltpu.get_barrier_semaphore()
    for d in range(1, TM):
        pl.semaphore_signal(barrier, inc=1, device_id={"tm": lax.rem(z + d, TM)}, device_id_type=MESH)
    for dy, dx in ((0, 1), (0, -1), (1, 0), (-1, 0)):
        pl.semaphore_signal(barrier, inc=1, device_id={"chan": chan_of(y + dy, x + dx, core)}, device_id_type=MESH)
    pl.semaphore_signal(barrier, inc=1, device_id={"chan": sibling}, device_id_type=MESH)

    def piece(p):
        return raw[pl.ds(p * HOP, HOP), :].astype(F32)

    fill_taper(taper)
    white[pl.ds(FULL * SPAN, 2 * SPAN), :] = jnp.zeros((2 * SPAN, CH), F32)
    for copy in loads[:2]:
        copy.wait()
    halo_out[...] = jnp.dot(
        table[2 * SPAN :, :], (piece(0) * (1.0 - taper[...])).astype(BF16), preferred_element_type=F32
    )

    waited = 1
    for pair in range(PIECES // 2):
        a, b = 2 * pair, 2 * pair + 1
        while waited < len(chunks) and b >= chunks[waited][0]:
            loads[1 + waited].wait()
            waited += 1
        one, two = piece(a), piece(b)
        up = jnp.concatenate([one * taper[...], two * taper[...]], axis=1).astype(BF16)
        first = jnp.dot(table[: 2 * SPAN, :], up, preferred_element_type=F32)
        spec[a] = first[:, :CH]
        spec[b] = first[:, CH:]
        fall = 1.0 - taper[...]
        down = jnp.concatenate([one * fall, two * fall], axis=1).astype(BF16)
        second = jnp.dot(table[2 * SPAN :, :], down, preferred_element_type=F32)
        if a > 0:
            spec[a - 1] = spec[a - 1] + second[:, :CH]
        spec[b - 1] = spec[b - 1] + second[:, CH:]

    pl.semaphore_wait(barrier, TM - 1 + 5)
    halo = pltpu.make_async_remote_copy(
        src_ref=halo_out, dst_ref=halo_in, send_sem=halo_sem.at[0], recv_sem=halo_sem.at[1],
        device_id={"tm": lax.rem(z + TM - 1, TM)}, device_id_type=MESH,
    )
    halo.start()

    def keep(k, spectra):
        real, imag = whiten(spectra)
        white[pl.ds(2 * k * SPAN, SPAN), :] = real
        white[pl.ds((2 * k + 1) * SPAN, SPAN), :] = imag

    for k in range(PIECES - 1):
        keep(k, spec[k])

    order = (1, -1, 2, -2, 3, -3, 4)
    sent = []

    def exchange(kind, out, into):
        for i, d in enumerate(order):
            target = lax.rem(z + d + TM, TM)
            if kind == 0:
                rows = [
                    white[pl.ds(SMOOTH + target * GROUP + b, ROWS, stride=SPAN), :] for b in range(GROUP)
                ]
            else:
                rows = [
                    white[pl.ds((FULL + part) * SPAN + SMOOTH + target * GROUP, 8), :] for part in range(2)
                ]
            out[i] = jnp.concatenate(rows, axis=0).astype(BF16)
            copy = pltpu.make_async_remote_copy(
                src_ref=out.at[i], dst_ref=into.at[z],
                send_sem=tm_send.at[kind, i], recv_sem=tm_recv.at[kind, z],
                device_id={"tm": target}, device_id_type=MESH,
            )
            copy.start()
            sent.append(copy)

    def received(kind, source, into):
        @pl.when(z != source)
        def _():
            pltpu.make_async_remote_copy(
                src_ref=into.at[source], dst_ref=into.at[source],
                send_sem=tm_send.at[kind, 0], recv_sem=tm_recv.at[kind, source],
                device_id={"tm": lax.rem(z + 1, TM)}, device_id_type=MESH,
            ).wait_recv()

    def unit(m, c, dp, dq, half=None):
        dy, dx = (dq, dp) if m == 0 else (dp, dq)
        yy, xx = lax.rem(y + dy + SIDE, SIDE), lax.rem(x + dx + SIDE, SIDE)
        return gathered.at[m, core, yy, xx, part_of(c, half)]

    def neighbour(m, axis, sign):
        along_x = (axis == "p") == (m == 0)
        return chan_of(y, x + sign, core) if along_x else chan_of(y + sign, x, core)

    slots = {}
    for side in (-1, 1):
        for kind in (None, 1):
            slots[("p", side, 0, kind)] = len(slots)
        for dp in (0, -1, 1, 2):
            for kind in (None, 1):
                slots[("q", side, dp, kind)] = len(slots)

    def copy_of(m, c, dp, dq, axis, side, half, to):
        slot = slots[(axis, side, dp if axis == "q" else 0, None if half is None else 1)]
        ref = unit(m, c, dp, dq, half)
        return pltpu.make_async_remote_copy(
            src_ref=ref, dst_ref=ref, send_sem=ici_send.at[m, 0 if axis == "p" else 1],
            recv_sem=ici_recv.at[m, c, slot],
            device_id={"chan": neighbour(m, axis, to)}, device_id_type=MESH,
        )

    def hand(m, c, dp, dq, axis, sign, half=None):
        copy_of(m, c, dp, dq, axis, -sign, half, sign).start()

    def arrive(m, c, dp, dq, axis, side, half=None):
        copy_of(m, c, dp, dq, axis, side, half, side).wait_recv()

    def share(m, c, dp, dq):
        ref = unit(m, c, dp, dq)
        pltpu.make_async_remote_copy(
            src_ref=ref, dst_ref=ref, send_sem=sib_send.at[m], recv_sem=sib_recv.at[m],
            device_id={"chan": sibling}, device_id_type=MESH,
        ).start()

    def own(c):
        for axis in ("p", "q"):
            for m in range(2):
                for sign in (1, -1):
                    hand(m, c, 0, 0, axis, sign)
        for m in range(2):
            share(m, c, 0, 0)

    def first_p(c):
        for side in (-1, 1):
            for m in range(2):
                arrive(m, c, side, 0, "p", side)
                hand(m, c, side, 0, "p", -side, half=0 if side < 0 else 1)
                hand(m, c, side, 0, "q", 1)
                hand(m, c, side, 0, "q", -1)
                share(m, c, side, 0)

    def second_p(c):
        for m in range(2):
            arrive(m, c, 2, 0, "p", -1, half=0)
            arrive(m, c, 2, 0, "p", 1, half=1)
            hand(m, c, 2, 0, "q", 1)
            hand(m, c, 2, 0, "q", -1)
            share(m, c, 2, 0)

    def first_q(c, dp):
        for side in (-1, 1):
            for m in range(2):
                arrive(m, c, dp, side, "q", side)
                hand(m, c, dp, side, "q", -side, half=0 if side < 0 else 1)
                share(m, c, dp, side)

    def second_q(c, dp):
        for m in range(2):
            arrive(m, c, dp, 2, "q", -1, half=0)
            arrive(m, c, dp, 2, "q", 1, half=1)
            share(m, c, dp, 2)

    def collect(c):
        for s in range(HALF):
            source = c * HALF + s
            received(0, source, from_tm)
            rows = from_tm[source].astype(F32)
            for b in range(GROUP):
                m, i = b // 2, b % 2
                start = (i * HALF + s) * FULL
                stage[m, start : start + FULL, :] = rows[b * ROWS : b * ROWS + FULL]
        for m in range(2):
            gathered[m, core, y, x, pl.ds(c * EARLY, EARLY), :] = stage[m].astype(BF16)

    def collect_last():
        for source in range(TM):
            received(1, source, from_last)
            last[16 * source : 16 * source + 16, :] = from_last[source].astype(F32)
        for m in range(2):
            rows = [last[pl.ds(2 * m + i, 2 * TM, stride=8), :] for i in range(2)]
            gathered[m, core, y, x, pl.ds(2 * EARLY, LAST), :] = jnp.concatenate(rows, axis=0).astype(BF16)

    def transpose_own():
        row = lax.broadcasted_iota(jnp.int32, (DEPTH, CH), 0)
        for b in range(GROUP):
            m, i = b // 2, b % 2
            rows = jnp.concatenate([gathered[m, core, y, x, part, :] for part in depth_of(i)], axis=0).astype(F32)
            other = EARLY // 2 if i == 0 else 0
            extra = CUT - EARLY // 2
            kept = True
            for start in (0, CUT):
                kept = kept & ((row < start + other) | (row >= start + other + extra))
            rows = jnp.where(kept, rows, 0.0)
            turned = jnp.where(lax.rem(row, 2) == 0, pltpu.roll(rows, DEPTH - 1, 0), -pltpu.roll(rows, 1, 0))
            own_t[b, :CH, :] = rows.T.astype(BF16)
            own_t[b, CH:, :] = turned.T.astype(BF16)

    exchange(0, to_tm, from_tm)
    from_tm[z] = jnp.concatenate(
        [white[pl.ds(SMOOTH + z * GROUP + b, ROWS, stride=SPAN), :] for b in range(GROUP)], axis=0
    ).astype(BF16)
    collect(0)
    own(0)
    halo.wait_recv()
    keep(PIECES - 1, spec[PIECES - 1] + jnp.where(z == TM - 1, 0.0, halo_in[...]))
    exchange(1, to_last, from_last)
    from_last[z] = jnp.concatenate(
        [white[pl.ds((FULL + part) * SPAN + SMOOTH + z * GROUP, 8), :] for part in range(2)], axis=0
    ).astype(BF16)
    first_p(0)
    collect(1)
    collect_last()
    own(1)
    first_q(0, 0)
    second_p(0)
    transpose_own()
    first_p(1)
    first_q(0, -1)
    first_q(0, 1)
    second_q(0, 0)
    first_q(1, 0)
    second_p(1)
    first_q(0, 2)
    second_q(0, -1)
    second_q(0, 1)
    first_q(1, -1)
    first_q(1, 1)
    second_q(1, 0)
    second_q(0, 2)
    first_q(1, 2)
    second_q(1, -1)
    second_q(1, 1)
    second_q(1, 2)

    halo.wait_send()
    for copy in sent:
        copy.wait_send()
    for m in range(2):
        for axis, all_sent in ((0, gathered.at[m, core, 0, pl.ds(0, 3)]), (1, gathered.at[m, core, pl.ds(0, 3)])):
            pltpu.make_async_remote_copy(
                src_ref=all_sent, dst_ref=all_sent, send_sem=ici_send.at[m, axis], recv_sem=ici_recv.at[m, 0, 0],
                device_id={"chan": sibling}, device_id_type=MESH,
            ).wait_send()
        shared = pltpu.make_async_remote_copy(
            src_ref=gathered.at[m, core], dst_ref=gathered.at[m, 1 - core],
            send_sem=sib_send.at[m], recv_sem=sib_recv.at[m],
            device_id={"chan": sibling}, device_id_type=MESH,
        )
        shared.wait_send()
        shared.wait_recv()


TILE = 4


def product_kernel(gathered, own_t, out, held, sems):
    steps = SIDE * SIDE // TILE
    wide = TILE * CORES * CH

    def copy_of(b, g):
        columns = pl.ds(pl.multiple_of(g * wide, wide), wide)
        return pltpu.make_async_copy(held.at[b, :, :, columns], out.at[b, :, :, columns], sems.at[b, g])

    def step(g, b):
        m, i = b // 2, b % 2
        for x in range(SIDE):
            right = jnp.concatenate(
                [jnp.concatenate([gathered[m, c, g, x, part, :] for part in depth_of(i)], axis=0) for c in range(CORES)],
                axis=1,
            )
            product = jnp.dot(own_t[b], right, preferred_element_type=F32) * (1.0 / FRAMES)
            product = product.astype(BF16)
            columns = pl.ds(pl.multiple_of(g * wide + x * CORES * CH, CORES * CH), CORES * CH)
            held[b, 0, :, columns] = product[:CH]
            held[b, 1, :, columns] = product[CH:]
        copy_of(b, g).start()

    for b in range(GROUP):
        @pl.loop(0, steps)
        def _(g):
            step(g, b)

    for b in range(GROUP):
        @pl.loop(0, steps)
        def _(g):
            copy_of(b, g).wait()


def local(raw_traces):
    any_space = pl.BlockSpec(memory_space=pl.ANY)
    vmem = pl.BlockSpec(memory_space=pltpu.VMEM)
    gathered, own_t = pl.pallas_call(
        gather_kernel,
        out_shape=(
            pltpu.VMEM((2, CORES, SIDE, SIDE, UNIT, CH), BF16),
            pltpu.VMEM((GROUP, 2 * CH, DEPTH), BF16),
        ),
        in_specs=[any_space] * 2,
        out_specs=(vmem, vmem),
        scratch_shapes=[
            pltpu.VMEM((PIECES * HOP, CH), BF16),
            pltpu.VMEM((4 * SPAN, HOP), BF16),
            pltpu.VMEM((HOP, CH), F32),
            pltpu.VMEM((PIECES, 2 * SPAN, CH), F32),
            pltpu.VMEM((2 * SPAN, CH), F32),
            pltpu.VMEM((2 * SPAN, CH), F32),
            pltpu.VMEM((ROWS * SPAN, CH), F32),
            pltpu.VMEM((TM - 1, GROUP * ROWS, CH), BF16),
            pltpu.VMEM((TM, GROUP * ROWS, CH), BF16),
            pltpu.VMEM((TM - 1, 16, CH), BF16),
            pltpu.VMEM((TM, 16, CH), BF16),
            pltpu.VMEM((16 * TM, CH), F32),
            pltpu.VMEM((2, EARLY, CH), F32),
            pltpu.SemaphoreType.DMA((5,)),
            pltpu.SemaphoreType.DMA((2,)),
            pltpu.SemaphoreType.DMA((2, TM - 1)),
            pltpu.SemaphoreType.DMA((2, TM)),
            pltpu.SemaphoreType.DMA((2, 2)),
            pltpu.SemaphoreType.DMA((2, 2, 20)),
            pltpu.SemaphoreType.DMA((2,)),
            pltpu.SemaphoreType.DMA((2,)),
        ],
        compiler_params=pltpu.CompilerParams(
            collective_id=0, has_side_effects=True, vmem_limit_bytes=24 * 1024 * 1024
        ),
    )(*(pltpu.with_memory_space_constraint(a, pltpu.HBM) for a in (raw_traces, spectral_table())))
    return pl.pallas_call(
        product_kernel,
        out_shape=jax.ShapeDtypeStruct((GROUP, 2, CH, SIDE * SIDE * CORES * CH), BF16),
        in_specs=[vmem, vmem],
        out_specs=any_space,
        scratch_shapes=[
            pltpu.VMEM((GROUP, 2, CH, SIDE * SIDE * CORES * CH), BF16),
            pltpu.SemaphoreType.DMA((GROUP, SIDE * SIDE // TILE)),
        ],
        compiler_params=pltpu.CompilerParams(vmem_limit_bytes=24 * 1024 * 1024),
    )(
        pltpu.with_memory_space_constraint(gathered, pltpu.VMEM),
        pltpu.with_memory_space_constraint(own_t, pltpu.VMEM),
    )


def solution(mesh):
    return jax.shard_map(
        local, mesh=mesh, in_specs=(P("tm", "chan"),), out_specs=P("tm", None, "chan", None), check_vma=False
    )
```

time: 62.4 us -> 48.3 us (0.77)
  Pallas kernels: 60.7 us -> 48.2 us
  local copies, waits for them, and re-layouts: 1.52 us -> 0 us
    pallas_call x1, Pallas kernels: 54.6 us -> 42.2 us  [local(): pl.pallas_call(gather_kernel, out_shape=(pltpu.VMEM((2, CORES, SIDE, SIDE...]
    another operation x1 -> x0, local copies, waits for them, and re-layouts: 1.52 us -> none
where the time goes in v3:
time: 48.3 us
  Pallas kernels  48.2 us (100%)
    pallas_call x1, Pallas kernels, local(): pl.pallas_call(gather_kernel, out_shape=(pltpu.VMEM((2, CORES, SIDE, SIDE...  42.2 us
    pallas_call x1, Pallas kernels, local(): pl.pallas_call(product_kernel, out_shape=jax.ShapeDtypeStruct((GROUP, 2,...  6.05 us

profile of v3, /device:TPU:1, one launch (start us, length us, event | category | flops | bytes accessed | tf_op | source)
XLA Modules:
  0.0 48.3 jit_solution(6558333727952909514)
XLA Ops:
  0.0 42.2 %shard_map.28 = (bf16[2,2,4,4,384,128]{5,4,3,2,1,0:T(8,128)(2,1)S(1)}, bf16[4,256,208]{2,1,0:T(8,128)(2,1)S(1)}) custom-call(bf16[6144,128]{1,0:T(8,128)(2,1)} %raw_hbm.1, bf16[160,512]{1,0:T(8,128)(2,1)} %constant.2.clone.table_hbm), custom_call_target="tpu_custom_call" | custom-call | tf_op jit(solution)/shard_map/pallas_call | solution.py:397
  42.2 6.1 %shard_map.29 = bf16[4,2,128,4096]{3,2,1,0:T(8,128)(2,1)} custom-call(bf16[2,2,4,4,384,128]{5,4,3,2,1,0:T(8,128)(2,1)S(1)} %get-tuple-element.7.gathered, bf16[4,256,208]{2,1,0:T(8,128)(2,1)S(1)} %get-tuple-element.8.own_t), custom_call_target="tpu_custom_call" | custom-call | tf_op jit(solution)/shard_map/pallas_call | solution.py:432

commit v4 on v3

v4 whole, which is shorter than its diff:
```python
import functools
import math

import jax
import jax.numpy as jnp
import numpy as np
from jax import lax
from jax.experimental import pallas as pl
from jax.experimental.pallas import tpu as pltpu
from jax.sharding import PartitionSpec as P

NFFT = 1024
HOP = NFFT // 2
NBINS = 32
SMOOTH = 4
BAND_START = 64
SPAN = NBINS + 2 * SMOOTH
FLOOR = 0.125 * math.sqrt(NFFT)
TM = 8
SIDE = 4
CORES = 2
CH = 128
PIECES = 12
FRAMES = TM * PIECES
GROUP = NBINS // TM
ROWS = 2 * PIECES
PARTS = 3
PART = ROWS // PARTS
LINES = TM * PART
CHUNK = 2 * LINES
UNIT = PARTS * CHUNK
DEPTH = PARTS * LINES
STRAIGHT = (False, False, False)
PLAN = ((0, 0), (1, 0), (2, 0), (0, 1), (1, 1), (2, 1), (0, 2), (1, 2), (0, 3), (2, 2), (1, 3), (2, 3), (0, 4), (1, 4), (2, 4))
MESH = pl.DeviceIdType.MESH
F32 = jnp.float32
BF16 = jnp.bfloat16


def spectral_table():
    sample = np.arange(NFFT)
    bins = BAND_START - SMOOTH + np.arange(SPAN)
    angles = (sample[:, None] * bins[None, :] % NFFT).astype(np.float64) * (2.0 * math.pi / NFFT)
    table = np.concatenate([np.cos(angles), -np.sin(angles)], axis=1).astype(np.float32)
    halves = np.concatenate([table[:HOP].T, table[HOP:].T], axis=0)
    return jnp.asarray(halves.astype(BF16))


def fill_taper(taper):
    step = 2.0 * math.pi / NFFT
    sample = lax.broadcasted_iota(jnp.int32, (8, CH), 0).astype(F32) * step
    cosine, sine = 0.5 * jnp.cos(sample), 0.5 * jnp.sin(sample)
    for i in range(HOP // 8):
        angle = 8 * i * step
        taper[8 * i : 8 * i + 8, :] = 0.5 - math.cos(angle) * cosine + math.sin(angle) * sine


def part_of(c, half=None):
    if half is None:
        return pl.ds(c * CHUNK, CHUNK)
    return pl.ds(c * CHUNK + half * LINES, LINES)


def depth_of(i):
    return [pl.ds(c * CHUNK + i * LINES, LINES) for c in range(PARTS)]


def whiten(spectra):
    real, imag = spectra[:SPAN], spectra[SPAN:]
    magnitude = jnp.sqrt(real * real + imag * imag)
    two = magnitude + pltpu.roll(magnitude, SPAN - 1, 0)
    four = two + pltpu.roll(two, SPAN - 2, 0)
    eight = four + pltpu.roll(four, SPAN - 4, 0)
    nine = eight + pltpu.roll(magnitude, SPAN - 8, 0)
    factor = 1.0 / jnp.maximum(nine * (1.0 / (2 * SMOOTH + 1)), FLOOR)
    factor = pltpu.roll(factor, SMOOTH, 0)
    return real * factor, imag * factor


def gather_kernel(
    raw_hbm, table_hbm, gathered, own_t,
    raw, table, taper, spec, halo_out, halo_in, white, to_tm, from_tm,
    load_sem, halo_sem, tm_send, tm_recv, ici_send, ici_recv, sib_send, sib_recv,
):
    z = lax.axis_index("tm")
    chan = lax.axis_index("chan")
    core = lax.rem(chan, CORES)
    place = chan // CORES
    y, x = place // SIDE, lax.rem(place, SIDE)

    def chan_of(yy, xx, cc):
        return (lax.rem(yy + SIDE, SIDE) * SIDE + lax.rem(xx + SIDE, SIDE)) * CORES + cc

    sibling = chan_of(y, x, 1 - core)

    chunks = [(0, 2), (2, 2), (4, 2), (6, 2), (8, 4)]
    loads = [pltpu.make_async_copy(table_hbm, table, load_sem.at[0])]
    for i, (first, count) in enumerate(chunks):
        part = pl.ds(first * HOP, count * HOP)
        loads.append(pltpu.make_async_copy(raw_hbm.at[part], raw.at[part], load_sem.at[1 + i]))
    for copy in loads:
        copy.start()

    barrier = pltpu.get_barrier_semaphore()
    for d in range(1, TM):
        pl.semaphore_signal(barrier, inc=1, device_id={"tm": lax.rem(z + d, TM)}, device_id_type=MESH)
    for dy, dx in ((0, 1), (0, -1), (1, 0), (-1, 0), (0, 2), (2, 0)):
        pl.semaphore_signal(barrier, inc=1, device_id={"chan": chan_of(y + dy, x + dx, core)}, device_id_type=MESH)
    pl.semaphore_signal(barrier, inc=1, device_id={"chan": sibling}, device_id_type=MESH)

    def piece(p):
        return raw[pl.ds(p * HOP, HOP), :].astype(F32)

    fill_taper(taper)
    loads[0].wait()
    loads[1].wait()
    halo_out[...] = jnp.dot(
        table[2 * SPAN :, :], (piece(0) * (1.0 - taper[...])).astype(BF16), preferred_element_type=F32
    )
    halo = pltpu.make_async_remote_copy(
        src_ref=halo_out, dst_ref=halo_in, send_sem=halo_sem.at[0], recv_sem=halo_sem.at[1],
        device_id={"tm": lax.rem(z + TM - 1, TM)}, device_id_type=MESH,
    )

    def enter():
        pl.semaphore_wait(barrier, TM - 1 + 7)
        halo.start()

    middle = (z >= 3) & (z <= 6)
    pl.when(middle)(enter)

    def keep(k, spectra):
        real, imag = whiten(spectra)
        white[pl.ds(2 * k * SPAN, SPAN), :] = real
        white[pl.ds((2 * k + 1) * SPAN, SPAN), :] = imag

    def transform(pair):
        a, b = 2 * pair, 2 * pair + 1
        one, two = piece(a), piece(b)
        up = jnp.concatenate([one * taper[...], two * taper[...]], axis=1).astype(BF16)
        first = jnp.dot(table[: 2 * SPAN, :], up, preferred_element_type=F32)
        spec[a] = first[:, :CH]
        spec[b] = first[:, CH:]
        fall = 1.0 - taper[...]
        down = jnp.concatenate([one * fall, two * fall], axis=1).astype(BF16)
        second = jnp.dot(table[2 * SPAN :, :], down, preferred_element_type=F32)
        if a > 0:
            spec[a - 1] = spec[a - 1] + second[:, :CH]
        spec[b - 1] = spec[b - 1] + second[:, CH:]

    order = (1, -1, 2, -2, 3, -3, 4)
    sent = []

    def rows_for(owner, c):
        rows = [
            white[pl.ds(c * PART * SPAN + SMOOTH + owner * GROUP + b, PART, stride=SPAN), :] for b in range(GROUP)
        ]
        return jnp.concatenate(rows, axis=0).astype(BF16)

    def exchange(c):
        for i, d in enumerate(order):
            target = lax.rem(z + d + TM, TM)
            to_tm[c, i] = rows_for(target, c)
            copy = pltpu.make_async_remote_copy(
                src_ref=to_tm.at[c, i], dst_ref=from_tm.at[c, z],
                send_sem=tm_send.at[c, i], recv_sem=tm_recv.at[c, z],
                device_id={"tm": target}, device_id_type=MESH,
            )
            copy.start()
            sent.append(copy)
        from_tm[c, z] = rows_for(z, c)

    def collect(c):
        for source in range(TM):
            @pl.when(z != source)
            def _():
                pltpu.make_async_remote_copy(
                    src_ref=from_tm.at[c, source], dst_ref=from_tm.at[c, source],
                    send_sem=tm_send.at[c, 0], recv_sem=tm_recv.at[c, source],
                    device_id={"tm": lax.rem(z + 1, TM)}, device_id_type=MESH,
                ).wait_recv()
        rows = [from_tm[c, source].astype(F32) for source in range(TM)]
        for b in range(GROUP):
            m, i = b // 2, b % 2
            whole = jnp.concatenate([part[b * PART : (b + 1) * PART] for part in rows], axis=0)
            gathered[m, core, y, x, pl.ds(c * CHUNK + i * LINES, LINES), :] = whole.astype(BF16)

    frames = PIECES // PARTS
    done = 0
    for pair in range(PIECES // 2):
        a, b = 2 * pair, 2 * pair + 1
        if 0 < pair < len(chunks):
            loads[1 + pair].wait()
        transform(pair)
        for c in range(PARTS - 1):
            if b - 1 >= (c + 1) * frames - 1 > a - 2:
                for k in range(c * frames, (c + 1) * frames):
                    keep(k, spec[k])
                if c == 0:
                    pl.when(jnp.logical_not(middle))(enter)
                exchange(c)
    for k in range((PARTS - 1) * frames, PIECES - 1):
        keep(k, spec[k])
    halo.wait_recv()
    keep(PIECES - 1, spec[PIECES - 1] + jnp.where(z == TM - 1, 0.0, halo_in[...]))
    exchange(PARTS - 1)

    def unit(m, c, dp, dq, half=None):
        dy, dx = (dq, dp) if m == 0 else (dp, dq)
        yy, xx = lax.rem(y + dy + SIDE, SIDE), lax.rem(x + dx + SIDE, SIDE)
        return gathered.at[m, core, yy, xx, part_of(c, half)]

    def neighbour(m, axis, sign):
        along_x = (axis == "p") == (m == 0)
        return chan_of(y, x + sign, core) if along_x else chan_of(y + sign, x, core)

    slots = {}
    for side in (-1, 1):
        for dp in (0, -1, 1, 2):
            for kind in (None, 1):
                slots[("q", side, dp, kind)] = len(slots)
    for side in (-1, 1, 2):
        slots[("p", side, 0, None)] = len(slots)
    for dp in (0, -1, 1, 2):
        slots[("q", 2, dp, None)] = len(slots)

    def copy_of(m, c, dp, dq, axis, side, half, to):
        slot = slots[(axis, side, dp if axis == "q" else 0, None if half is None else 1)]
        ref = unit(m, c, dp, dq, half)
        return pltpu.make_async_remote_copy(
            src_ref=ref, dst_ref=ref, send_sem=ici_send.at[m, 0 if axis == "p" else 1],
            recv_sem=ici_recv.at[m, c, slot],
            device_id={"chan": neighbour(m, axis, to)}, device_id_type=MESH,
        )

    def hand(m, c, dp, dq, axis, sign, half=None):
        copy_of(m, c, dp, dq, axis, sign if sign == 2 else -sign, half, sign).start()

    def arrive(m, c, dp, dq, axis, side, half=None):
        copy_of(m, c, dp, dq, axis, side, half, side).wait_recv()

    def share(m, c, dp, dq):
        ref = unit(m, c, dp, dq)
        pltpu.make_async_remote_copy(
            src_ref=ref, dst_ref=ref, send_sem=sib_send.at[m], recv_sem=sib_recv.at[m],
            device_id={"chan": sibling}, device_id_type=MESH,
        ).start()

    def own(c):
        for m in range(2):
            for sign in (2, 1, -1):
                hand(m, c, 0, 0, "p", sign)
        for m in range(2):
            to_q(m, c, 0)
        for m in range(2):
            share(m, c, 0, 0)

    def to_q(m, c, dp):
        for sign in (2, 1, -1) if STRAIGHT[c] else (1, -1):
            hand(m, c, dp, 0, "q", sign)

    def across(c, dp):
        for m in range(2):
            arrive(m, c, dp, 0, "p", dp)
            to_q(m, c, dp)
            share(m, c, dp, 0)

    def first_q(c, dp):
        for side in (-1, 1):
            for m in range(2):
                arrive(m, c, dp, side, "q", side)
                if not STRAIGHT[c]:
                    hand(m, c, dp, side, "q", -side, half=0 if side < 0 else 1)
                share(m, c, dp, side)

    def second_q(c, dp):
        for m in range(2):
            if STRAIGHT[c]:
                arrive(m, c, dp, 2, "q", 2)
            else:
                arrive(m, c, dp, 2, "q", -1, half=0)
                arrive(m, c, dp, 2, "q", 1, half=1)
            share(m, c, dp, 2)

    def stage(c, k):
        if k == 0:
            collect(c)
            own(c)
        elif k == 1:
            for dp in (-1, 1, 2):
                across(c, dp)
        elif k == 2:
            first_q(c, 0)
        elif k == 3:
            for dp in (-1, 1, 2):
                first_q(c, dp)
        else:
            for dp in (0, -1, 1, 2):
                second_q(c, dp)

    def transpose_own():
        row = lax.broadcasted_iota(jnp.int32, (DEPTH, CH), 0)
        for b in range(GROUP):
            m, i = b // 2, b % 2
            rows = jnp.concatenate([gathered[m, core, y, x, part, :] for part in depth_of(i)], axis=0).astype(F32)
            turned = jnp.where(lax.rem(row, 2) == 0, pltpu.roll(rows, DEPTH - 1, 0), -pltpu.roll(rows, 1, 0))
            own_t[b, :CH, :] = rows.T.astype(BF16)
            own_t[b, CH:, :] = turned.T.astype(BF16)

    for c, k in PLAN:
        stage(c, k)
        if (c, k) == (0, 4):
            transpose_own()

    halo.wait_send()
    for copy in sent:
        copy.wait_send()
    for m in range(2):
        for axis, all_sent in ((0, gathered.at[m, core, 0, pl.ds(0, 3)]), (1, gathered.at[m, core, pl.ds(0, 3)])):
            pltpu.make_async_remote_copy(
                src_ref=all_sent, dst_ref=all_sent, send_sem=ici_send.at[m, axis], recv_sem=ici_recv.at[m, 0, 0],
                device_id={"chan": sibling}, device_id_type=MESH,
            ).wait_send()
        shared = pltpu.make_async_remote_copy(
            src_ref=gathered.at[m, core], dst_ref=gathered.at[m, 1 - core],
            send_sem=sib_send.at[m], recv_sem=sib_recv.at[m],
            device_id={"chan": sibling}, device_id_type=MESH,
        )
        shared.wait_send()
        shared.wait_recv()


TILE = 4


def product_kernel(gathered, own_t, out, held, sems):
    steps = SIDE * SIDE // TILE
    wide = TILE * CORES * CH

    def copy_of(b, g):
        columns = pl.ds(pl.multiple_of(g * wide, wide), wide)
        return pltpu.make_async_copy(held.at[b, :, :, columns], out.at[b, :, :, columns], sems.at[b, g])

    def step(g, b):
        m, i = b // 2, b % 2
        for x in range(SIDE):
            right = jnp.concatenate(
                [jnp.concatenate([gathered[m, c, g, x, part, :] for part in depth_of(i)], axis=0) for c in range(CORES)],
                axis=1,
            )
            product = jnp.dot(own_t[b], right, preferred_element_type=F32) * (1.0 / FRAMES)
            product = product.astype(BF16)
            columns = pl.ds(pl.multiple_of(g * wide + x * CORES * CH, CORES * CH), CORES * CH)
            held[b, 0, :, columns] = product[:CH]
            held[b, 1, :, columns] = product[CH:]
        copy_of(b, g).start()

    for b in range(GROUP):
        @pl.loop(0, steps)
        def _(g):
            step(g, b)

    for b in range(GROUP):
        @pl.loop(0, steps)
        def _(g):
            copy_of(b, g).wait()


def local(raw_traces):
    any_space = pl.BlockSpec(memory_space=pl.ANY)
    vmem = pl.BlockSpec(memory_space=pltpu.VMEM)
    gathered, own_t = pl.pallas_call(
        gather_kernel,
        out_shape=(
            pltpu.VMEM((2, CORES, SIDE, SIDE, UNIT, CH), BF16),
            pltpu.VMEM((GROUP, 2 * CH, DEPTH), BF16),
        ),
        in_specs=[any_space] * 2,
        out_specs=(vmem, vmem),
        scratch_shapes=[
            pltpu.VMEM((PIECES * HOP, CH), BF16),
            pltpu.VMEM((4 * SPAN, HOP), BF16),
            pltpu.VMEM((HOP, CH), F32),
            pltpu.VMEM((PIECES, 2 * SPAN, CH), F32),
            pltpu.VMEM((2 * SPAN, CH), F32),
            pltpu.VMEM((2 * SPAN, CH), F32),
            pltpu.VMEM((ROWS * SPAN, CH), F32),
            pltpu.VMEM((PARTS, TM - 1, GROUP * PART, CH), BF16),
            pltpu.VMEM((PARTS, TM, GROUP * PART, CH), BF16),
            pltpu.SemaphoreType.DMA((6,)),
            pltpu.SemaphoreType.DMA((2,)),
            pltpu.SemaphoreType.DMA((PARTS, TM - 1)),
            pltpu.SemaphoreType.DMA((PARTS, TM)),
            pltpu.SemaphoreType.DMA((2, 2)),
            pltpu.SemaphoreType.DMA((2, PARTS, 23)),
            pltpu.SemaphoreType.DMA((2,)),
            pltpu.SemaphoreType.DMA((2,)),
        ],
        compiler_params=pltpu.CompilerParams(
            collective_id=0, has_side_effects=True, vmem_limit_bytes=24 * 1024 * 1024
        ),
    )(*(pltpu.with_memory_space_constraint(a, pltpu.HBM) for a in (raw_traces, spectral_table())))
    return pl.pallas_call(
        product_kernel,
        out_shape=jax.ShapeDtypeStruct((GROUP, 2, CH, SIDE * SIDE * CORES * CH), BF16),
        in_specs=[vmem, vmem],
        out_specs=any_space,
        scratch_shapes=[
            pltpu.VMEM((GROUP, 2, CH, SIDE * SIDE * CORES * CH), BF16),
            pltpu.SemaphoreType.DMA((GROUP, SIDE * SIDE // TILE)),
        ],
        compiler_params=pltpu.CompilerParams(vmem_limit_bytes=24 * 1024 * 1024),
    )(
        pltpu.with_memory_space_constraint(gathered, pltpu.VMEM),
        pltpu.with_memory_space_constraint(own_t, pltpu.VMEM),
    )


def solution(mesh):
    return jax.shard_map(
        local, mesh=mesh, in_specs=(P("tm", "chan"),), out_specs=P("tm", None, "chan", None), check_vma=False
    )
```

time: 48.3 us -> 43.8 us (0.907)
  Pallas kernels: 48.2 us -> 43.7 us
    pallas_call x1, Pallas kernels: 42.2 us -> 37.7 us  [local(): pl.pallas_call(gather_kernel, out_shape=(pltpu.VMEM((2, CORES, SIDE, SIDE...]
where the time goes in v4:
time: 43.8 us; the launch traced here: 43.7 us
  Pallas kernels  43.7 us (100%)
    pallas_call x1, Pallas kernels, local(): pl.pallas_call(gather_kernel, out_shape=(pltpu.VMEM((2, CORES, SIDE, SIDE...  37.7 us
    pallas_call x1, Pallas kernels, local(): pl.pallas_call(product_kernel, out_shape=jax.ShapeDtypeStruct((GROUP, 2,...  5.99 us

profile of v4, /device:TPU:1, one launch (start us, length us, event | category | flops | bytes accessed | tf_op | source)
XLA Modules:
  0.0 43.7 jit_solution(2955193046676598110)
XLA Ops:
  0.0 37.7 %shard_map.28 = (bf16[2,2,4,4,384,128]{5,4,3,2,1,0:T(8,128)(2,1)S(1)}, bf16[4,256,192]{2,1,0:T(8,128)(2,1)S(1)}) custom-call(bf16[6144,128]{1,0:T(8,128)(2,1)} %raw_hbm.1, bf16[160,512]{1,0:T(8,128)(2,1)} %constant.2.clone.table_hbm), custom_call_target="tpu_custom_call" | custom-call | tf_op jit(solution)/shard_map/pallas_call | solution.py:372
  37.7 6.0 %shard_map.29 = bf16[4,2,128,4096]{3,2,1,0:T(8,128)(2,1)} custom-call(bf16[2,2,4,4,384,128]{5,4,3,2,1,0:T(8,128)(2,1)S(1)} %get-tuple-element.7.gathered, bf16[4,256,192]{2,1,0:T(8,128)(2,1)S(1)} %get-tuple-element.8.own_t), custom_call_target="tpu_custom_call" | custom-call | tf_op jit(solution)/shard_map/pallas_call | solution.py:403

commit v5 on v4

--- a/solution.py
+++ b/solution.py
@@ -330,40 +330,26 @@
         shared.wait_recv()
 
 
-TILE = 4
-
-
 def product_kernel(gathered, own_t, out, held, sems):
-    steps = SIDE * SIDE // TILE
-    wide = TILE * CORES * CH
-
-    def copy_of(b, g):
-        columns = pl.ds(pl.multiple_of(g * wide, wide), wide)
-        return pltpu.make_async_copy(held.at[b, :, :, columns], out.at[b, :, :, columns], sems.at[b, g])
-
-    def step(g, b):
+    wide = CORES * CH
+    copies = []
+    for b in range(GROUP):
         m, i = b // 2, b % 2
-        for x in range(SIDE):
+        for place in range(SIDE * SIDE):
+            yy, xx = place // SIDE, place % SIDE
             right = jnp.concatenate(
-                [jnp.concatenate([gathered[m, c, g, x, part, :] for part in depth_of(i)], axis=0) for c in range(CORES)],
+                [jnp.concatenate([gathered[m, c, yy, xx, part, :] for part in depth_of(i)], axis=0) for c in range(CORES)],
                 axis=1,
             )
             product = jnp.dot(own_t[b], right, preferred_element_type=F32) * (1.0 / FRAMES)
             product = product.astype(BF16)
-            columns = pl.ds(pl.multiple_of(g * wide + x * CORES * CH, CORES * CH), CORES * CH)
+            columns = slice(place * wide, place * wide + wide)
             held[b, 0, :, columns] = product[:CH]
             held[b, 1, :, columns] = product[CH:]
-        copy_of(b, g).start()
-
-    for b in range(GROUP):
-        @pl.loop(0, steps)
-        def _(g):
-            step(g, b)
-
-    for b in range(GROUP):
-        @pl.loop(0, steps)
-        def _(g):
-            copy_of(b, g).wait()
+        copies.append(pltpu.make_async_copy(held.at[b], out.at[b], sems.at[b]))
+        copies[-1].start()
+    for copy in copies:
+        copy.wait()
 
 
 def local(raw_traces):
@@ -407,7 +393,7 @@
         out_specs=any_space,
         scratch_shapes=[
             pltpu.VMEM((GROUP, 2, CH, SIDE * SIDE * CORES * CH), BF16),
-            pltpu.SemaphoreType.DMA((GROUP, SIDE * SIDE // TILE)),
+            pltpu.SemaphoreType.DMA((GROUP,)),
         ],
         compiler_params=pltpu.CompilerParams(vmem_limit_bytes=24 * 1024 * 1024),
     )(

time: 43.8 us -> 41.9 us (0.957)
  Pallas kernels: 43.7 us -> 41.8 us
    pallas_call x1, Pallas kernels: 5.99 us -> 4.07 us  [local(): pl.pallas_call(product_kernel, out_shape=jax.ShapeDtypeStruct((GROUP, 2,...]
where the time goes in v5:
time: 41.9 us; the launch traced here: 41.8 us
  Pallas kernels  41.8 us (100%)
    pallas_call x1, Pallas kernels, local(): pl.pallas_call(gather_kernel, out_shape=(pltpu.VMEM((2, CORES, SIDE, SIDE...  37.7 us
    pallas_call x1, Pallas kernels, local(): pl.pallas_call(product_kernel, out_shape=jax.ShapeDtypeStruct((GROUP, 2,...  4.07 us

profile of v5, /device:TPU:1, one launch (start us, length us, event | category | flops | bytes accessed | tf_op | source)
XLA Modules:
  0.0 41.8 jit_solution(8357244286405872006)
XLA Ops:
  0.0 37.7 %shard_map.28 = (bf16[2,2,4,4,384,128]{5,4,3,2,1,0:T(8,128)(2,1)S(1)}, bf16[4,256,192]{2,1,0:T(8,128)(2,1)S(1)}) custom-call(bf16[6144,128]{1,0:T(8,128)(2,1)} %raw_hbm.1, bf16[160,512]{1,0:T(8,128)(2,1)} %constant.2.clone.table_hbm), custom_call_target="tpu_custom_call" | custom-call | tf_op jit(solution)/shard_map/pallas_call | solution.py:358
  37.7 4.1 %shard_map.29 = bf16[4,2,128,4096]{3,2,1,0:T(8,128)(2,1)} custom-call(bf16[2,2,4,4,384,128]{5,4,3,2,1,0:T(8,128)(2,1)S(1)} %get-tuple-element.7.gathered, bf16[4,256,192]{2,1,0:T(8,128)(2,1)S(1)} %get-tuple-element.8.own_t), custom_call_target="tpu_custom_call" | custom-call | tf_op jit(solution)/shard_map/pallas_call | solution.py:389

commit v6 on v5

--- a/solution.py
+++ b/solution.py
@@ -24,14 +24,13 @@
 FRAMES = TM * PIECES
 GROUP = NBINS // TM
 ROWS = 2 * PIECES
-PARTS = 3
-PART = ROWS // PARTS
-LINES = TM * PART
-CHUNK = 2 * LINES
-UNIT = PARTS * CHUNK
-DEPTH = PARTS * LINES
-STRAIGHT = (False, False, False)
-PLAN = ((0, 0), (1, 0), (2, 0), (0, 1), (1, 1), (2, 1), (0, 2), (1, 2), (0, 3), (2, 2), (1, 3), (2, 3), (0, 4), (1, 4), (2, 4))
+FIRST = 16
+PARTS = (FIRST, ROWS - FIRST)
+LINES = tuple(part * TM for part in PARTS)
+STARTS = tuple(2 * sum(LINES[:c]) for c in range(len(LINES)))
+UNIT = 2 * sum(LINES)
+DEPTH = sum(LINES)
+PLAN = tuple((c, stage) for stage in range(5) for c in range(len(PARTS)))
 MESH = pl.DeviceIdType.MESH
 F32 = jnp.float32
 BF16 = jnp.bfloat16
@@ -57,12 +56,12 @@
 
 def part_of(c, half=None):
     if half is None:
-        return pl.ds(c * CHUNK, CHUNK)
-    return pl.ds(c * CHUNK + half * LINES, LINES)
+        return pl.ds(STARTS[c], 2 * LINES[c])
+    return pl.ds(STARTS[c] + half * LINES[c], LINES[c])
 
 
 def depth_of(i):
-    return [pl.ds(c * CHUNK + i * LINES, LINES) for c in range(PARTS)]
+    return [part_of(c, i) for c in range(len(PARTS))]
 
 
 def whiten(spectra):
@@ -93,7 +92,7 @@
 
     sibling = chan_of(y, x, 1 - core)
 
-    chunks = [(0, 2), (2, 2), (4, 2), (6, 2), (8, 4)]
+    chunks = [(0, 2), (2, 4), (6, 6)]
     loads = [pltpu.make_async_copy(table_hbm, table, load_sem.at[0])]
     for i, (first, count) in enumerate(chunks):
         part = pl.ds(first * HOP, count * HOP)
@@ -126,7 +125,7 @@
         pl.semaphore_wait(barrier, TM - 1 + 7)
         halo.start()
 
-    middle = (z >= 3) & (z <= 6)
+    middle = (z >= 4) & (z <= 6)
     pl.when(middle)(enter)
 
     def keep(k, spectra):
@@ -148,62 +147,54 @@
             spec[a - 1] = spec[a - 1] + second[:, :CH]
         spec[b - 1] = spec[b - 1] + second[:, CH:]
 
-    order = (1, -1, 2, -2, 3, -3, 4)
-    sent = []
-
-    def rows_for(owner, c):
-        rows = [
-            white[pl.ds(c * PART * SPAN + SMOOTH + owner * GROUP + b, PART, stride=SPAN), :] for b in range(GROUP)
-        ]
+    order = (4, 3, -3, 2, -2, 1, -1)
+
+    def rows_for(owner, part):
+        first = (part * FIRST) * SPAN + SMOOTH + owner * GROUP
+        rows = [white[pl.ds(first + b, PARTS[part], stride=SPAN), :] for b in range(GROUP)]
         return jnp.concatenate(rows, axis=0).astype(BF16)
 
-    def exchange(c):
+    def exchange(part):
+        count = pl.ds(0, GROUP * PARTS[part])
         for i, d in enumerate(order):
             target = lax.rem(z + d + TM, TM)
-            to_tm[c, i] = rows_for(target, c)
+            to_tm[part, i, count, :] = rows_for(target, part)
             copy = pltpu.make_async_remote_copy(
-                src_ref=to_tm.at[c, i], dst_ref=from_tm.at[c, z],
-                send_sem=tm_send.at[c, i], recv_sem=tm_recv.at[c, z],
+                src_ref=to_tm.at[part, i, count], dst_ref=from_tm.at[part, z, count],
+                send_sem=tm_send.at[part], recv_sem=tm_recv.at[part],
                 device_id={"tm": target}, device_id_type=MESH,
             )
             copy.start()
-            sent.append(copy)
-        from_tm[c, z] = rows_for(z, c)
-
-    def collect(c):
-        for source in range(TM):
-            @pl.when(z != source)
-            def _():
-                pltpu.make_async_remote_copy(
-                    src_ref=from_tm.at[c, source], dst_ref=from_tm.at[c, source],
-                    send_sem=tm_send.at[c, 0], recv_sem=tm_recv.at[c, source],
-                    device_id={"tm": lax.rem(z + 1, TM)}, device_id_type=MESH,
-                ).wait_recv()
-        rows = [from_tm[c, source].astype(F32) for source in range(TM)]
+        from_tm[part, z, count, :] = rows_for(z, part)
+
+    def collect(part):
+        lines, count = PARTS[part], pl.ds(0, GROUP * PARTS[part])
+        ref = from_tm.at[part, pl.ds(0, TM - 1), count]
+        pltpu.make_async_remote_copy(
+            src_ref=ref, dst_ref=ref, send_sem=tm_send.at[part], recv_sem=tm_recv.at[part],
+            device_id={"tm": lax.rem(z + 1, TM)}, device_id_type=MESH,
+        ).wait_recv()
+        rows = [from_tm[part, source, count, :].astype(F32) for source in range(TM)]
         for b in range(GROUP):
             m, i = b // 2, b % 2
-            whole = jnp.concatenate([part[b * PART : (b + 1) * PART] for part in rows], axis=0)
-            gathered[m, core, y, x, pl.ds(c * CHUNK + i * LINES, LINES), :] = whole.astype(BF16)
-
-    frames = PIECES // PARTS
-    done = 0
+            whole = jnp.concatenate([block[b * lines : (b + 1) * lines] for block in rows], axis=0)
+            gathered[m, core, y, x, part_of(part, i), :] = whole.astype(BF16)
+
     for pair in range(PIECES // 2):
-        a, b = 2 * pair, 2 * pair + 1
-        if 0 < pair < len(chunks):
-            loads[1 + pair].wait()
+        for i, (first, count) in enumerate(chunks):
+            if i > 0 and first == 2 * pair:
+                loads[1 + i].wait()
         transform(pair)
-        for c in range(PARTS - 1):
-            if b - 1 >= (c + 1) * frames - 1 > a - 2:
-                for k in range(c * frames, (c + 1) * frames):
-                    keep(k, spec[k])
-                if c == 0:
-                    pl.when(jnp.logical_not(middle))(enter)
-                exchange(c)
-    for k in range((PARTS - 1) * frames, PIECES - 1):
+        if pair == FIRST // 4:
+            for k in range(FIRST // 2):
+                keep(k, spec[k])
+            pl.when(jnp.logical_not(middle))(enter)
+            exchange(0)
+    for k in range(FIRST // 2, PIECES - 1):
         keep(k, spec[k])
     halo.wait_recv()
     keep(PIECES - 1, spec[PIECES - 1] + jnp.where(z == TM - 1, 0.0, halo_in[...]))
-    exchange(PARTS - 1)
+    exchange(1)
 
     def unit(m, c, dp, dq, half=None):
         dy, dx = (dq, dp) if m == 0 else (dp, dq)
@@ -214,30 +205,25 @@
         along_x = (axis == "p") == (m == 0)
         return chan_of(y, x + sign, core) if along_x else chan_of(y + sign, x, core)
 
-    slots = {}
-    for side in (-1, 1):
-        for dp in (0, -1, 1, 2):
-            for kind in (None, 1):
-                slots[("q", side, dp, kind)] = len(slots)
-    for side in (-1, 1, 2):
-        slots[("p", side, 0, None)] = len(slots)
-    for dp in (0, -1, 1, 2):
-        slots[("q", 2, dp, None)] = len(slots)
-
-    def copy_of(m, c, dp, dq, axis, side, half, to):
-        slot = slots[(axis, side, dp if axis == "q" else 0, None if half is None else 1)]
+    def slot_of(axis, dp, half):
+        if axis == "p":
+            return 1 if dp == 2 else 0
+        return (2 if half is None else 5) + abs(dp)
+
+    def hand(m, c, dp, dq, axis, sign, half=None):
         ref = unit(m, c, dp, dq, half)
-        return pltpu.make_async_remote_copy(
+        pltpu.make_async_remote_copy(
             src_ref=ref, dst_ref=ref, send_sem=ici_send.at[m, 0 if axis == "p" else 1],
-            recv_sem=ici_recv.at[m, c, slot],
-            device_id={"chan": neighbour(m, axis, to)}, device_id_type=MESH,
-        )
-
-    def hand(m, c, dp, dq, axis, sign, half=None):
-        copy_of(m, c, dp, dq, axis, sign if sign == 2 else -sign, half, sign).start()
-
-    def arrive(m, c, dp, dq, axis, side, half=None):
-        copy_of(m, c, dp, dq, axis, side, half, side).wait_recv()
+            recv_sem=ici_recv.at[c, slot_of(axis, sign if axis == "p" else dp, half)],
+            device_id={"chan": neighbour(m, axis, sign)}, device_id_type=MESH,
+        ).start()
+
+    def settle(c, axis, dp, units, half=None):
+        ref = gathered.at[:, core, 0, pl.ds(0, units), part_of(c)]
+        pltpu.make_async_remote_copy(
+            src_ref=ref, dst_ref=ref, send_sem=ici_send.at[0, 0], recv_sem=ici_recv.at[c, slot_of(axis, dp, half)],
+            device_id={"chan": sibling}, device_id_type=MESH,
+        ).wait_recv()
 
     def share(m, c, dp, dq):
         ref = unit(m, c, dp, dq)
@@ -256,47 +242,46 @@
             share(m, c, 0, 0)
 
     def to_q(m, c, dp):
-        for sign in (2, 1, -1) if STRAIGHT[c] else (1, -1):
+        for sign in (1, -1):
             hand(m, c, dp, 0, "q", sign)
 
-    def across(c, dp):
-        for m in range(2):
-            arrive(m, c, dp, 0, "p", dp)
-            to_q(m, c, dp)
-            share(m, c, dp, 0)
-
-    def first_q(c, dp):
-        for side in (-1, 1):
+    def across(c, dps):
+        settle(c, "p", dps[0], len(dps))
+        for dp in dps:
             for m in range(2):
-                arrive(m, c, dp, side, "q", side)
-                if not STRAIGHT[c]:
+                to_q(m, c, dp)
+                share(m, c, dp, 0)
+
+    def first_q(c, dps):
+        settle(c, "q", dps[0], 2 * len(dps))
+        for dp in dps:
+            for side in (-1, 1):
+                for m in range(2):
                     hand(m, c, dp, side, "q", -side, half=0 if side < 0 else 1)
-                share(m, c, dp, side)
-
-    def second_q(c, dp):
-        for m in range(2):
-            if STRAIGHT[c]:
-                arrive(m, c, dp, 2, "q", 2)
-            else:
-                arrive(m, c, dp, 2, "q", -1, half=0)
-                arrive(m, c, dp, 2, "q", 1, half=1)
-            share(m, c, dp, 2)
+                    share(m, c, dp, side)
+
+    def second_q(c, dps):
+        settle(c, "q", dps[0], len(dps), 1)
+        for dp in dps:
+            for m in range(2):
+                share(m, c, dp, 2)
 
     def stage(c, k):
         if k == 0:
             collect(c)
             own(c)
         elif k == 1:
-            for dp in (-1, 1, 2):
-                across(c, dp)
+            across(c, (-1, 1))
+            across(c, (2,))
         elif k == 2:
-            first_q(c, 0)
+            first_q(c, (0,))
         elif k == 3:
-            for dp in (-1, 1, 2):
-                first_q(c, dp)
+            first_q(c, (-1, 1))
+            first_q(c, (2,))
         else:
-            for dp in (0, -1, 1, 2):
-                second_q(c, dp)
+            second_q(c, (0,))
+            second_q(c, (-1, 1))
+            second_q(c, (2,))
 
     def transpose_own():
         row = lax.broadcasted_iota(jnp.int32, (DEPTH, CH), 0)
@@ -313,12 +298,16 @@
             transpose_own()
 
     halo.wait_send()
-    for copy in sent:
-        copy.wait_send()
+    for part in range(2):
+        ref = to_tm.at[part, :, pl.ds(0, GROUP * PARTS[part])]
+        pltpu.make_async_remote_copy(
+            src_ref=ref, dst_ref=ref, send_sem=tm_send.at[part], recv_sem=tm_recv.at[part],
+            device_id={"tm": lax.rem(z + 1, TM)}, device_id_type=MESH,
+        ).wait_send()
     for m in range(2):
         for axis, all_sent in ((0, gathered.at[m, core, 0, pl.ds(0, 3)]), (1, gathered.at[m, core, pl.ds(0, 3)])):
             pltpu.make_async_remote_copy(
-                src_ref=all_sent, dst_ref=all_sent, send_sem=ici_send.at[m, axis], recv_sem=ici_recv.at[m, 0, 0],
+                src_ref=all_sent, dst_ref=all_sent, send_sem=ici_send.at[m, axis], recv_sem=ici_recv.at[0, 0],
                 device_id={"chan": sibling}, device_id_type=MESH,
             ).wait_send()
         shared = pltpu.make_async_remote_copy(
@@ -371,14 +360,14 @@
             pltpu.VMEM((2 * SPAN, CH), F32),
             pltpu.VMEM((2 * SPAN, CH), F32),
             pltpu.VMEM((ROWS * SPAN, CH), F32),
-            pltpu.VMEM((PARTS, TM - 1, GROUP * PART, CH), BF16),
-            pltpu.VMEM((PARTS, TM, GROUP * PART, CH), BF16),
-            pltpu.SemaphoreType.DMA((6,)),
+            pltpu.VMEM((2, TM - 1, GROUP * FIRST, CH), BF16),
+            pltpu.VMEM((2, TM, GROUP * FIRST, CH), BF16),
+            pltpu.SemaphoreType.DMA((4,)),
             pltpu.SemaphoreType.DMA((2,)),
-            pltpu.SemaphoreType.DMA((PARTS, TM - 1)),
-            pltpu.SemaphoreType.DMA((PARTS, TM)),
+            pltpu.SemaphoreType.DMA((2,)),
+            pltpu.SemaphoreType.DMA((len(PARTS),)),
             pltpu.SemaphoreType.DMA((2, 2)),
-            pltpu.SemaphoreType.DMA((2, PARTS, 23)),
+            pltpu.SemaphoreType.DMA((len(PARTS), 8)),
             pltpu.SemaphoreType.DMA((2,)),
             pltpu.SemaphoreType.DMA((2,)),
         ],

time: 41.9 us -> 40.4 us (0.964)
  Pallas kernels: 41.8 us -> 40.3 us
    pallas_call x1, Pallas kernels: 37.7 us -> 36.2 us  [local(): pl.pallas_call(gather_kernel, out_shape=(pltpu.VMEM((2, CORES, SIDE, SIDE...]
where the time goes in v6:
time: 40.4 us; the launch traced here: 40.3 us
  Pallas kernels  40.3 us (100%)
    pallas_call x1, Pallas kernels, local(): pl.pallas_call(gather_kernel, out_shape=(pltpu.VMEM((2, CORES, SIDE, SIDE...  36.2 us
    pallas_call x1, Pallas kernels, local(): pl.pallas_call(product_kernel, out_shape=jax.ShapeDtypeStruct((GROUP, 2,...  4.07 us

profile of v6, /device:TPU:1, one launch (start us, length us, event | category | flops | bytes accessed | tf_op | source)
XLA Modules:
  0.0 40.3 jit_solution(7608794483587443442)
XLA Ops:
  0.0 36.2 %shard_map.28 = (bf16[2,2,4,4,384,128]{5,4,3,2,1,0:T(8,128)(2,1)S(1)}, bf16[4,256,192]{2,1,0:T(8,128)(2,1)S(1)}) custom-call(bf16[6144,128]{1,0:T(8,128)(2,1)} %raw_hbm.1, bf16[160,512]{1,0:T(8,128)(2,1)} %constant.2.clone.table_hbm), custom_call_target="tpu_custom_call" | custom-call | tf_op jit(solution)/shard_map/pallas_call | solution.py:347
  36.2 4.1 %shard_map.29 = bf16[4,2,128,4096]{3,2,1,0:T(8,128)(2,1)} custom-call(bf16[2,2,4,4,384,128]{5,4,3,2,1,0:T(8,128)(2,1)S(1)} %get-tuple-element.7.gathered, bf16[4,256,192]{2,1,0:T(8,128)(2,1)S(1)} %get-tuple-element.8.own_t), custom_call_target="tpu_custom_call" | custom-call | tf_op jit(solution)/shard_map/pallas_call | solution.py:378

commit v7 on v6

--- a/solution.py
+++ b/solution.py
@@ -24,8 +24,8 @@
 FRAMES = TM * PIECES
 GROUP = NBINS // TM
 ROWS = 2 * PIECES
-FIRST = 16
-PARTS = (FIRST, ROWS - FIRST)
+FIRST = 8
+PARTS = (8, 8, 8)
 LINES = tuple(part * TM for part in PARTS)
 STARTS = tuple(2 * sum(LINES[:c]) for c in range(len(LINES)))
 UNIT = 2 * sum(LINES)
@@ -126,7 +126,6 @@
         halo.start()
 
     middle = (z >= 4) & (z <= 6)
-    pl.when(middle)(enter)
 
     def keep(k, spectra):
         real, imag = whiten(spectra)
@@ -185,16 +184,18 @@
             if i > 0 and first == 2 * pair:
                 loads[1 + i].wait()
         transform(pair)
-        if pair == FIRST // 4:
-            for k in range(FIRST // 2):
+        if pair in (2, 4):
+            part = pair // 2 - 1
+            for k in range(4 * part, 4 * part + 4):
                 keep(k, spec[k])
-            pl.when(jnp.logical_not(middle))(enter)
-            exchange(0)
-    for k in range(FIRST // 2, PIECES - 1):
+            if part == 0:
+                enter()
+            exchange(part)
+    for k in range(8, PIECES - 1):
         keep(k, spec[k])
     halo.wait_recv()
     keep(PIECES - 1, spec[PIECES - 1] + jnp.where(z == TM - 1, 0.0, halo_in[...]))
-    exchange(1)
+    exchange(2)
 
     def unit(m, c, dp, dq, half=None):
         dy, dx = (dq, dp) if m == 0 else (dp, dq)
@@ -298,7 +299,7 @@
             transpose_own()
 
     halo.wait_send()
-    for part in range(2):
+    for part in range(3):
         ref = to_tm.at[part, :, pl.ds(0, GROUP * PARTS[part])]
         pltpu.make_async_remote_copy(
             src_ref=ref, dst_ref=ref, send_sem=tm_send.at[part], recv_sem=tm_recv.at[part],
@@ -360,11 +361,11 @@
             pltpu.VMEM((2 * SPAN, CH), F32),
             pltpu.VMEM((2 * SPAN, CH), F32),
             pltpu.VMEM((ROWS * SPAN, CH), F32),
-            pltpu.VMEM((2, TM - 1, GROUP * FIRST, CH), BF16),
-            pltpu.VMEM((2, TM, GROUP * FIRST, CH), BF16),
+            pltpu.VMEM((3, TM - 1, GROUP * FIRST, CH), BF16),
+            pltpu.VMEM((3, TM, GROUP * FIRST, CH), BF16),
             pltpu.SemaphoreType.DMA((4,)),
             pltpu.SemaphoreType.DMA((2,)),
-            pltpu.SemaphoreType.DMA((2,)),
+            pltpu.SemaphoreType.DMA((3,)),
             pltpu.SemaphoreType.DMA((len(PARTS),)),
             pltpu.SemaphoreType.DMA((2, 2)),
             pltpu.SemaphoreType.DMA((len(PARTS), 8)),

time: 40.4 us -> 40.2 us (level)
  no operation moved by 1% of the time
where the time goes in v7:
time: 40.2 us; the launch traced here: 40.1 us
  Pallas kernels  40.1 us (100%)
    pallas_call x1, Pallas kernels, local(): pl.pallas_call(gather_kernel, out_shape=(pltpu.VMEM((2, CORES, SIDE, SIDE...  36 us
    pallas_call x1, Pallas kernels, local(): pl.pallas_call(product_kernel, out_shape=jax.ShapeDtypeStruct((GROUP, 2,...  4.07 us

profile of v7, /device:TPU:1, one launch (start us, length us, event | category | flops | bytes accessed | tf_op | source)
XLA Modules:
  0.0 40.1 jit_solution(3231215844208502718)
XLA Ops:
  0.0 36.0 %shard_map.28 = (bf16[2,2,4,4,384,128]{5,4,3,2,1,0:T(8,128)(2,1)S(1)}, bf16[4,256,192]{2,1,0:T(8,128)(2,1)S(1)}) custom-call(bf16[6144,128]{1,0:T(8,128)(2,1)} %raw_hbm.1, bf16[160,512]{1,0:T(8,128)(2,1)} %constant.2.clone.table_hbm), custom_call_target="tpu_custom_call" | custom-call | tf_op jit(solution)/shard_map/pallas_call | solution.py:348
  36.0 4.1 %shard_map.29 = bf16[4,2,128,4096]{3,2,1,0:T(8,128)(2,1)} custom-call(bf16[2,2,4,4,384,128]{5,4,3,2,1,0:T(8,128)(2,1)S(1)} %get-tuple-element.7.gathered, bf16[4,256,192]{2,1,0:T(8,128)(2,1)S(1)} %get-tuple-element.8.own_t), custom_call_target="tpu_custom_call" | custom-call | tf_op jit(solution)/shard_map/pallas_call | solution.py:379

commit v8 on v7

--- a/solution.py
+++ b/solution.py
@@ -77,7 +77,7 @@
 
 
 def gather_kernel(
-    raw_hbm, table_hbm, gathered, own_t,
+    raw_hbm, table_hbm, gathered, own_t, held,
     raw, table, taper, spec, halo_out, halo_in, white, to_tm, from_tm,
     load_sem, halo_sem, tm_send, tm_recv, ici_send, ici_recv, sib_send, sib_recv,
 ):
@@ -97,15 +97,15 @@
     for i, (first, count) in enumerate(chunks):
         part = pl.ds(first * HOP, count * HOP)
         loads.append(pltpu.make_async_copy(raw_hbm.at[part], raw.at[part], load_sem.at[1 + i]))
-    for copy in loads:
-        copy.start()
-
     barrier = pltpu.get_barrier_semaphore()
     for d in range(1, TM):
         pl.semaphore_signal(barrier, inc=1, device_id={"tm": lax.rem(z + d, TM)}, device_id_type=MESH)
     for dy, dx in ((0, 1), (0, -1), (1, 0), (-1, 0), (0, 2), (2, 0)):
         pl.semaphore_signal(barrier, inc=1, device_id={"chan": chan_of(y + dy, x + dx, core)}, device_id_type=MESH)
     pl.semaphore_signal(barrier, inc=1, device_id={"chan": sibling}, device_id_type=MESH)
+
+    for copy in loads:
+        copy.start()
 
     def piece(p):
         return raw[pl.ds(p * HOP, HOP), :].astype(F32)
@@ -229,9 +229,16 @@
     def share(m, c, dp, dq):
         ref = unit(m, c, dp, dq)
         pltpu.make_async_remote_copy(
-            src_ref=ref, dst_ref=ref, send_sem=sib_send.at[m], recv_sem=sib_recv.at[m],
+            src_ref=ref, dst_ref=ref, send_sem=sib_send.at[0], recv_sem=sib_recv.at[abs(dq)],
             device_id={"chan": sibling}, device_id_type=MESH,
         ).start()
+
+    def shared(dq):
+        ref = gathered.at[:, 1 - core, pl.ds(0, 2 if dq == 1 else 1)]
+        pltpu.make_async_remote_copy(
+            src_ref=ref, dst_ref=ref, send_sem=sib_send.at[0], recv_sem=sib_recv.at[dq],
+            device_id={"chan": sibling}, device_id_type=MESH,
+        ).wait_recv()
 
     def own(c):
         for m in range(2):
@@ -295,8 +302,15 @@
 
     for c, k in PLAN:
         stage(c, k)
-        if (c, k) == (0, 4):
+        if (c, k) == (len(PARTS) - 1, 2):
             transpose_own()
+        if (c, k) == (len(PARTS) - 1, 3):
+            shared(0)
+            products(gathered, own_t, held, y, x, 0)
+        if (c, k) == (len(PARTS) - 2, 4):
+            shared(1)
+            products(gathered, own_t, held, y, x, -1)
+    products(gathered, own_t, held, y, x, 1)
 
     halo.wait_send()
     for part in range(3):
@@ -311,31 +325,38 @@
                 src_ref=all_sent, dst_ref=all_sent, send_sem=ici_send.at[m, axis], recv_sem=ici_recv.at[0, 0],
                 device_id={"chan": sibling}, device_id_type=MESH,
             ).wait_send()
-        shared = pltpu.make_async_remote_copy(
-            src_ref=gathered.at[m, core], dst_ref=gathered.at[m, 1 - core],
-            send_sem=sib_send.at[m], recv_sem=sib_recv.at[m],
-            device_id={"chan": sibling}, device_id_type=MESH,
-        )
-        shared.wait_send()
-        shared.wait_recv()
-
-
-def product_kernel(gathered, own_t, out, held, sems):
+    ref = gathered.at[:, core]
+    pltpu.make_async_remote_copy(
+        src_ref=ref, dst_ref=ref, send_sem=sib_send.at[0], recv_sem=sib_recv.at[0],
+        device_id={"chan": sibling}, device_id_type=MESH,
+    ).wait_send()
+    shared(2)
+
+
+def products(gathered, own_t, held, y, x, dq, bins=tuple(range(GROUP))):
     wide = CORES * CH
-    copies = []
-    for b in range(GROUP):
-        m, i = b // 2, b % 2
-        for place in range(SIDE * SIDE):
-            yy, xx = place // SIDE, place % SIDE
+
+    for along in range(SIDE):
+        for b in bins:
+            m, i = b // 2, b % 2
+            yy, xx = (lax.rem(y + dq + SIDE, SIDE), along) if m == 0 else (along, lax.rem(x + dq + SIDE, SIDE))
             right = jnp.concatenate(
                 [jnp.concatenate([gathered[m, c, yy, xx, part, :] for part in depth_of(i)], axis=0) for c in range(CORES)],
                 axis=1,
             )
             product = jnp.dot(own_t[b], right, preferred_element_type=F32) * (1.0 / FRAMES)
             product = product.astype(BF16)
-            columns = slice(place * wide, place * wide + wide)
+            columns = pl.ds(pl.multiple_of((yy * SIDE + xx) * wide, wide), wide)
             held[b, 0, :, columns] = product[:CH]
             held[b, 1, :, columns] = product[CH:]
+
+
+def product_kernel(gathered, own_t, most, out, held, sems):
+    place = lax.axis_index("chan") // CORES
+    y, x = place // SIDE, lax.rem(place, SIDE)
+    copies = []
+    for b in range(GROUP):
+        products(gathered, own_t, held, y, x, 2, (b,))
         copies.append(pltpu.make_async_copy(held.at[b], out.at[b], sems.at[b]))
         copies[-1].start()
     for copy in copies:
@@ -345,14 +366,16 @@
 def local(raw_traces):
     any_space = pl.BlockSpec(memory_space=pl.ANY)
     vmem = pl.BlockSpec(memory_space=pltpu.VMEM)
-    gathered, own_t = pl.pallas_call(
+    result = (GROUP, 2, CH, SIDE * SIDE * CORES * CH)
+    gathered, own_t, held = pl.pallas_call(
         gather_kernel,
         out_shape=(
             pltpu.VMEM((2, CORES, SIDE, SIDE, UNIT, CH), BF16),
             pltpu.VMEM((GROUP, 2 * CH, DEPTH), BF16),
+            pltpu.VMEM(result, BF16),
         ),
         in_specs=[any_space] * 2,
-        out_specs=(vmem, vmem),
+        out_specs=(vmem, vmem, vmem),
         scratch_shapes=[
             pltpu.VMEM((PIECES * HOP, CH), BF16),
             pltpu.VMEM((4 * SPAN, HOP), BF16),
@@ -369,27 +392,23 @@
             pltpu.SemaphoreType.DMA((len(PARTS),)),
             pltpu.SemaphoreType.DMA((2, 2)),
             pltpu.SemaphoreType.DMA((len(PARTS), 8)),
-            pltpu.SemaphoreType.DMA((2,)),
-            pltpu.SemaphoreType.DMA((2,)),
+            pltpu.SemaphoreType.DMA((1,)),
+            pltpu.SemaphoreType.DMA((3,)),
         ],
         compiler_params=pltpu.CompilerParams(
             collective_id=0, has_side_effects=True, vmem_limit_bytes=24 * 1024 * 1024
         ),
     )(*(pltpu.with_memory_space_constraint(a, pltpu.HBM) for a in (raw_traces, spectral_table())))
-    return pl.pallas_call(
+    out, _ = pl.pallas_call(
         product_kernel,
-        out_shape=jax.ShapeDtypeStruct((GROUP, 2, CH, SIDE * SIDE * CORES * CH), BF16),
-        in_specs=[vmem, vmem],
-        out_specs=any_space,
-        scratch_shapes=[
-            pltpu.VMEM((GROUP, 2, CH, SIDE * SIDE * CORES * CH), BF16),
-            pltpu.SemaphoreType.DMA((GROUP,)),
-        ],
+        out_shape=(jax.ShapeDtypeStruct(result, BF16), pltpu.VMEM(result, BF16)),
+        in_specs=[vmem] * 3,
+        out_specs=(any_space, vmem),
+        input_output_aliases={2: 1},
+        scratch_shapes=[pltpu.SemaphoreType.DMA((GROUP,))],
         compiler_params=pltpu.CompilerParams(vmem_limit_bytes=24 * 1024 * 1024),
-    )(
-        pltpu.with_memory_space_constraint(gathered, pltpu.VMEM),
-        pltpu.with_memory_space_constraint(own_t, pltpu.VMEM),
-    )
+    )(*(pltpu.with_memory_space_constraint(array, pltpu.VMEM) for array in (gathered, own_t, held)))
+    return out
 
 
 def solution(mesh):

time: 40.2 us -> 39.8 us (0.990)
  no operation moved by 1% of the time
where the time goes in v8:
time: 39.8 us; the launch traced here: 39.7 us
  Pallas kernels  39.7 us (100%)
    pallas_call x1, Pallas kernels, local(): pl.pallas_call(gather_kernel, out_shape=(pltpu.VMEM((2, CORES, SIDE, SIDE...  36 us
    pallas_call x1, Pallas kernels, local(): pl.pallas_call(product_kernel, out_shape=(jax.ShapeDtypeStruct(result, BF...  3.69 us

profile of v8, /device:TPU:1, one launch (start us, length us, event | category | flops | bytes accessed | tf_op | source)
XLA Modules:
  0.0 39.7 jit_solution(6149675084114286097)
XLA Ops:
  0.0 36.0 %shard_map.28 = (bf16[2,2,4,4,384,128]{5,4,3,2,1,0:T(8,128)(2,1)S(1)}, bf16[4,256,192]{2,1,0:T(8,128)(2,1)S(1)}, bf16[4,2,128,4096]{3,2,1,0:T(8,128)(2,1)S(1)}) custom-call(bf16[6144,128]{1,0:T(8,128)(2,1)} %raw_hbm.1, bf16[160,512]{1,0:T(8,128)(2,1)} %constant.2.clone.table_hbm), custom_call_target="tpu_custom_call" | custom-call | tf_op jit(solution)/shard_map/pallas_call | solution.py:370
  36.0 3.7 %shard_map.29 = (bf16[4,2,128,4096]{3,2,1,0:T(8,128)(2,1)}, bf16[4,2,128,4096]{3,2,1,0:T(8,128)(2,1)S(1)}) custom-call(bf16[2,2,4,4,384,128]{5,4,3,2,1,0:T(8,128)(2,1)S(1)} %get-tuple-element.9.gathered, bf16[4,256,192]{2,1,0:T(8,128)(2,1)S(1)} %get-tuple-element.10.own_t, ...), custom_call_target="tpu_custom_call", output_to_operand_aliasing={{1}: (2, {})} | custom-call | tf_op jit(solution)/shard_map/pallas_call | solution.py:402

commit v9 on v8

--- a/solution.py
+++ b/solution.py
@@ -383,7 +383,7 @@
             pltpu.VMEM((PIECES, 2 * SPAN, CH), F32),
             pltpu.VMEM((2 * SPAN, CH), F32),
             pltpu.VMEM((2 * SPAN, CH), F32),
-            pltpu.VMEM((ROWS * SPAN, CH), F32),
+            pltpu.VMEM(((ROWS + 1) * SPAN, CH), F32),
             pltpu.VMEM((3, TM - 1, GROUP * FIRST, CH), BF16),
             pltpu.VMEM((3, TM, GROUP * FIRST, CH), BF16),
             pltpu.SemaphoreType.DMA((4,)),

time: 39.8 us -> 39.8 us (level)
  no operation moved by 1% of the time
where the time goes in v9:
time: 39.8 us; the launch traced here: 39.7 us
  Pallas kernels  39.7 us (100%)
    pallas_call x1, Pallas kernels, local(): pl.pallas_call(gather_kernel, out_shape=(pltpu.VMEM((2, CORES, SIDE, SIDE...  36 us
    pallas_call x1, Pallas kernels, local(): pl.pallas_call(product_kernel, out_shape=(jax.ShapeDtypeStruct(result, BF...  3.69 us

profile of v9, /device:TPU:1, one launch (start us, length us, event | category | flops | bytes accessed | tf_op | source)
XLA Modules:
  0.0 39.7 jit_solution(5021896311518235712)
XLA Ops:
  0.0 36.0 %shard_map.28 = (bf16[2,2,4,4,384,128]{5,4,3,2,1,0:T(8,128)(2,1)S(1)}, bf16[4,256,192]{2,1,0:T(8,128)(2,1)S(1)}, bf16[4,2,128,4096]{3,2,1,0:T(8,128)(2,1)S(1)}) custom-call(bf16[6144,128]{1,0:T(8,128)(2,1)} %raw_hbm.1, bf16[160,512]{1,0:T(8,128)(2,1)} %constant.2.clone.table_hbm), custom_call_target="tpu_custom_call" | custom-call | tf_op jit(solution)/shard_map/pallas_call | solution.py:370
  36.0 3.7 %shard_map.29 = (bf16[4,2,128,4096]{3,2,1,0:T(8,128)(2,1)}, bf16[4,2,128,4096]{3,2,1,0:T(8,128)(2,1)S(1)}) custom-call(bf16[2,2,4,4,384,128]{5,4,3,2,1,0:T(8,128)(2,1)S(1)} %get-tuple-element.9.gathered, bf16[4,256,192]{2,1,0:T(8,128)(2,1)S(1)} %get-tuple-element.10.own_t, ...), custom_call_target="tpu_custom_call", output_to_operand_aliasing={{1}: (2, {})} | custom-call | tf_op jit(solution)/shard_map/pallas_call | solution.py:402
